TPU v7x, 32 devices: a whole 2x2x4 slice. The times are simulated.
32 devices in a mesh: dp: 16 (over z, y, x), mp: 2 (over core).
Axes of the slice: x: 2, y: 2, z: 4, core: 2. Of those that a mesh axis runs over, the one named last changes fastest.
Arguments:
- tokens: bfloat16 [6144, 1024], P('dp'), may hold values from -6 to 6
- cotangent: bfloat16 [6144, 1024], P('dp'), may hold values from -6 to 6
- qkv_weight: bfloat16 [3, 1024, 1024], P(None, None, 'mp'), may hold values from -0.1875 to 0.1875
- out_weight: bfloat16 [1024, 1024], P('mp'), may hold values from -4 to 4
- up_weight: bfloat16 [1024, 4096], P(None, 'mp'), may hold values from -0.1875 to 0.1875
- down_weight: bfloat16 [4096, 1024], P('mp'), may hold values from -0.09375 to 0.09375
- norm_gain: float32 [2, 8, 1024], replicated, may hold values from 0.5 to 1.5
- norm_shift: float32 [2, 8, 1024], replicated, may hold values from -1.25 to 1.25
- lengths: int32 [16], P('dp'), may hold values from 192 to 384, as said below
- prompt_src: int32 [16], P('dp'), may hold values from 0 to 15, as said below
- prompt_len: int32 [16], P('dp'), may hold values from 48 to 96, as said below
- codebook_section: int32 [16], P('dp'), may hold values from 1 to 7
- adam_step: int32 [1], replicated, may hold values from 1 to 4
- master: float32 [2, 6307840], P('mp', 'dp')
- first_moment: float32 [2, 6307840], P('mp', 'dp')
- second_moment: float32 [2, 6307840], P('mp', 'dp'), as said below
- ema_weight: float32 [2, 6307840], P('mp', 'dp')
Outputs:
- block_out: bfloat16 [6144, 1024], P('dp')
- input_grad: bfloat16 [6144, 1024], P('dp')
- grad_norm: float32 [1], replicated
- new_first: float32 [2, 6307840], P('mp', 'dp')
- new_second: float32 [2, 6307840], P('mp', 'dp')
- new_master: float32 [2, 6307840], P('mp', 'dp')
- master_copy: bfloat16 [2, 6307840], P('mp', 'dp')
- new_ema: float32 [2, 6307840], P('mp', 'dp')
Inputs may be any that keep to these rules, and one draw needn't show every extreme that they name: `lengths`: valid frames at the start of each utterance's 384 slots; some utterance fills them all. `prompt_src`: another utterance of the same speaker group; speaker groups are aligned runs of four dp indices or halves of such runs, and the first run is one group. `prompt_len`: frames taken from the start of the source utterance; some utterance takes 96. `second_moment`: positive.
All inputs are finite; a program needn't handle non-finite values.
Results may differ from a plain program's by a relative error of at most 0.015.
Values may be sent and summed in bfloat16 or wider, within the bound.
No kernel may reach another device: no remote copies, remote signals or barrier semaphores. Data moves between devices by JAX's collectives and lax.ppermute only.
A program may use at most 192 MiB of HBM per device.

v0:
```python
import jax
import jax.numpy as jnp
from jax import lax
from jax.sharding import PartitionSpec as P

D = 1024
HDIM = 64
FF = 4096
SECTIONS = 8
TOK_DEV = 384
QBLOCK = 384
PMAX = 96
OUT_FAN = 2


CLIP_NORM = 1.0
BETA_ONE = 0.5
BETA_TWO = 0.5
WEIGHT_DECAY = 0.1
EMA_DECAY = 0.75


def passed_along(value, axis, steps):
    count = lax.axis_size(axis)
    leading, last = (max(0, -steps), min(count, count - steps))
    return lax.ppermute(value, axis, [(source, source + steps) for source in range(leading, last)])


def normalize(values, gain_row, shift_row):
    centred = values - jnp.mean(values, axis=-1, keepdims=True)
    variance = jnp.mean(centred * centred, axis=-1, keepdims=True)
    return gain_row * (centred * lax.rsqrt(variance + 1e-05)) + shift_row


def gelu_exact(values):
    return jax.nn.gelu(values, approximate=False)


def score_block(query_block, key_all, key_ok):
    scores = jnp.einsum(
        "qhe,khe->hqk", query_block, key_all, preferred_element_type=jnp.float32
    ) * HDIM ** (-0.5)
    return jnp.where(key_ok[None, None, :], scores, -1e30)


def as_rows(matrix, splits):
    return matrix.reshape(splits, -1)


def body(
    tokens,
    cotangent,
    qkv_weight,
    out_weight,
    up_weight,
    down_weight,
    norm_gain,
    norm_shift,
    lengths,
    prompt_src,
    prompt_len,
    codebook_section,
    adam_step,
    master,
    first_moment,
    second_moment,
    ema_weight,
):
    dp_index = lax.axis_index("dp")
    mp_index = lax.axis_index("mp")
    dp_count = lax.axis_size("dp")
    half_width = qkv_weight.shape[2]
    heads_here = half_width // HDIM
    block_count = TOK_DEV // QBLOCK
    valid_length = lengths[0]
    source = prompt_src[0]
    prompt_count = prompt_len[0]
    selector = (jnp.arange(SECTIONS) == codebook_section[0]).astype(jnp.float32)
    table = jnp.stack([norm_gain[0], norm_shift[0], norm_gain[1], norm_shift[1]])
    section_rows = jnp.einsum("s,ksd->kd", selector, table, precision=lax.Precision.HIGHEST)
    inputs = tokens.astype(jnp.float32)
    normed_first, first_pull = jax.vjp(normalize, inputs, section_rows[0], section_rows[1])
    normed_low = normed_first.astype(jnp.bfloat16)
    projected = jnp.einsum(
        "td,cde->cte", normed_low, qkv_weight, preferred_element_type=jnp.float32
    ).astype(jnp.bfloat16)
    own_prompt = projected[1:, :PMAX]
    offset = dp_index - source
    prompt_pair = jnp.zeros_like(own_prompt)
    for distance in (-3, -2, -1, 1, 2, 3):
        arrived = passed_along(own_prompt, "dp", distance)
        prompt_pair = jnp.where(offset == distance, arrived, prompt_pair)
    key_all = jnp.concatenate([projected[1], prompt_pair[0]], axis=0).reshape(-1, heads_here, HDIM)
    value_all = jnp.concatenate([projected[2], prompt_pair[1]], axis=0).reshape(
        -1, heads_here, HDIM
    )
    positions = jnp.arange(TOK_DEV + PMAX)
    key_ok = jnp.where(
        positions < TOK_DEV, positions < valid_length, positions - TOK_DEV < prompt_count
    )
    query_blocks = projected[0].reshape(block_count, QBLOCK, heads_here, HDIM)

    def attend(query_block):
        scores = score_block(query_block, key_all, key_ok)
        row_max = jnp.max(scores, axis=2, keepdims=True)
        exponent = jnp.exp(scores - row_max)
        row_total = jnp.sum(exponent, axis=2, keepdims=True)
        probability = (exponent / row_total).astype(jnp.bfloat16)
        mixed = jnp.einsum(
            "hqk,khe->qhe", probability, value_all, preferred_element_type=jnp.float32
        )
        return (mixed.astype(jnp.bfloat16), (row_max + jnp.log(row_total))[..., 0])

    attended, log_totals = lax.map(attend, query_blocks)
    attended_flat = attended.reshape(TOK_DEV, half_width)
    branch_out = lax.psum(
        jnp.dot(attended_flat, out_weight, preferred_element_type=jnp.float32).astype(jnp.bfloat16),
        "mp",
    ).astype(jnp.float32)
    hidden_state = inputs + branch_out
    normed_second, second_pull = jax.vjp(normalize, hidden_state, section_rows[2], section_rows[3])
    second_low = normed_second.astype(jnp.bfloat16)
    pre_act = jnp.dot(second_low, up_weight, preferred_element_type=jnp.float32)
    activated, gelu_pull = jax.vjp(gelu_exact, pre_act)
    act_low = activated.astype(jnp.bfloat16)
    ffn_out = lax.psum(
        jnp.dot(act_low, down_weight, preferred_element_type=jnp.float32).astype(jnp.bfloat16), "mp"
    ).astype(jnp.float32)
    block_out = (hidden_state + ffn_out).astype(jnp.bfloat16)
    row_ok = (jnp.arange(TOK_DEV) < valid_length).astype(jnp.float32)[:, None]
    grad_out = cotangent.astype(jnp.float32) * row_ok
    grad_low = grad_out.astype(jnp.bfloat16)
    grad_down = jnp.dot(act_low.T, grad_low, preferred_element_type=jnp.float32)
    grad_act = jnp.dot(grad_low, down_weight.T, preferred_element_type=jnp.float32)
    pre_low = gelu_pull(grad_act)[0].astype(jnp.bfloat16)
    grad_up = jnp.dot(second_low.T, pre_low, preferred_element_type=jnp.float32)
    grad_second = lax.psum(
        jnp.dot(pre_low, up_weight.T, preferred_element_type=jnp.float32).astype(jnp.bfloat16), "mp"
    ).astype(jnp.float32)
    hidden_back, gain_two, shift_two = second_pull(grad_second)
    grad_hidden = grad_out + hidden_back
    hidden_low = grad_hidden.astype(jnp.bfloat16)
    grad_outproj = jnp.dot(attended_flat.T, hidden_low, preferred_element_type=jnp.float32)
    grad_attended = jnp.dot(hidden_low, out_weight.T, preferred_element_type=jnp.float32).astype(
        jnp.bfloat16
    )
    grad_blocks = grad_attended.reshape(block_count, QBLOCK, heads_here, HDIM)

    def revisit(carried, block_inputs):
        key_grad, value_grad = carried
        query_block, grad_block, log_block = block_inputs
        scores = score_block(query_block, key_all, key_ok)
        probability = jnp.exp(scores - log_block[..., None])
        value_grad = value_grad + jnp.einsum(
            "hqk,qhe->khe",
            probability.astype(jnp.bfloat16),
            grad_block,
            preferred_element_type=jnp.float32,
        )
        grad_prob = jnp.einsum(
            "qhe,khe->hqk", grad_block, value_all, preferred_element_type=jnp.float32
        )
        centre = jnp.sum(probability * grad_prob, axis=2, keepdims=True)
        grad_scores = (probability * (grad_prob - centre)).astype(jnp.bfloat16)
        query_grad = jnp.einsum(
            "hqk,khe->qhe", grad_scores, key_all, preferred_element_type=jnp.float32
        ) * HDIM ** (-0.5)
        key_grad = key_grad + jnp.einsum(
            "hqk,qhe->khe", grad_scores, query_block, preferred_element_type=jnp.float32
        ) * HDIM ** (-0.5)
        return ((key_grad, value_grad), query_grad)

    zero_rows = jnp.zeros((TOK_DEV + PMAX, heads_here, HDIM), jnp.float32)
    (key_grad, value_grad), query_grads = lax.scan(
        revisit, (zero_rows, zero_rows), (query_blocks, grad_blocks, log_totals)
    )
    key_flat = key_grad.reshape(TOK_DEV + PMAX, half_width)
    value_flat = value_grad.reshape(TOK_DEV + PMAX, half_width)
    local_grads = jnp.stack(
        [query_grads.reshape(TOK_DEV, half_width), key_flat[:TOK_DEV], value_flat[:TOK_DEV]]
    ).astype(jnp.bfloat16)
    sent_back = jnp.stack([key_flat[TOK_DEV:], value_flat[TOK_DEV:]]).astype(jnp.bfloat16)
    nothing_sent = jnp.zeros_like(sent_back)
    returned = jnp.zeros(sent_back.shape, jnp.float32)
    for distance in (-3, -2, -1, 1, 2, 3):
        outgoing = jnp.where(offset == distance, sent_back, nothing_sent)
        returned = returned + passed_along(outgoing, "dp", -distance).astype(jnp.float32)
    returned_low = returned.astype(jnp.bfloat16)
    grad_qkv = jnp.einsum(
        "td,cte->cde", normed_low, local_grads, preferred_element_type=jnp.float32
    )
    prompt_part = jnp.einsum(
        "td,cte->cde", normed_low[:PMAX], returned_low, preferred_element_type=jnp.float32
    )
    grad_qkv = jnp.concatenate([grad_qkv[:1], grad_qkv[1:] + prompt_part], axis=0)
    grad_normed = jnp.einsum(
        "cte,cde->td", local_grads, qkv_weight, preferred_element_type=jnp.float32
    )
    prompt_back = jnp.einsum(
        "cte,cde->td", returned_low, qkv_weight[1:], preferred_element_type=jnp.float32
    )
    grad_normed = grad_normed + jnp.pad(prompt_back, ((0, TOK_DEV - PMAX), (0, 0)))
    grad_normed = lax.psum(grad_normed.astype(jnp.bfloat16), "mp").astype(jnp.float32)
    input_back, gain_one, shift_one = first_pull(grad_normed)
    input_grad = (grad_hidden + input_back).astype(jnp.bfloat16)
    gain_table = selector[None, :, None] * jnp.stack([gain_one, gain_two])[:, None, :]
    shift_table = selector[None, :, None] * jnp.stack([shift_one, shift_two])[:, None, :]
    gain_half = lax.dynamic_slice_in_dim(gain_table, mp_index * half_width, half_width, 2)
    shift_half = lax.dynamic_slice_in_dim(shift_table, mp_index * half_width, half_width, 2)
    reduced = (
        lax.psum_scatter(as_rows(grad_qkv, dp_count), "dp", scatter_dimension=0, tiled=True),
        lax.psum_scatter(as_rows(grad_outproj, dp_count), "dp", scatter_dimension=0, tiled=True),
        lax.psum_scatter(as_rows(grad_up, dp_count), "dp", scatter_dimension=0, tiled=True),
        lax.psum_scatter(as_rows(grad_down, dp_count), "dp", scatter_dimension=0, tiled=True),
        lax.psum_scatter(as_rows(gain_half, dp_count), "dp", scatter_dimension=0, tiled=True),
        lax.psum_scatter(as_rows(shift_half, dp_count), "dp", scatter_dimension=0, tiled=True),
    )
    pieces = list(reduced)
    gradient = jnp.concatenate(pieces, axis=1)
    square_sum = lax.psum(jnp.sum(gradient * gradient), ("dp", "mp"))
    grad_norm = jnp.sqrt(square_sum)
    clip_scale = jnp.minimum(1.0, CLIP_NORM / (grad_norm + 1e-06))
    rates = [D ** (-0.5), OUT_FAN ** (-0.5), D ** (-0.5), FF ** (-0.5), 0.2, 0.2]
    rate_row = jnp.concatenate(
        [
            jnp.full((piece_item.shape[1],), rate_item, jnp.float32)
            for piece_item, rate_item in zip(pieces, rates)
        ]
    )[None, :]
    clipped = clip_scale * gradient
    new_first = BETA_ONE * first_moment + (1.0 - BETA_ONE) * clipped
    new_second = BETA_TWO * second_moment + (1.0 - BETA_TWO) * clipped * clipped
    step_count = adam_step[0].astype(jnp.float32)
    first_fix = 1.0 - jnp.power(BETA_ONE, step_count)
    second_fix = 1.0 - jnp.power(BETA_TWO, step_count)
    update = new_first / first_fix / (jnp.sqrt(new_second / second_fix) + 1e-08)
    new_master = master - rate_row * (update + WEIGHT_DECAY * master)
    new_ema = EMA_DECAY * ema_weight + (1.0 - EMA_DECAY) * new_master
    return (
        block_out,
        input_grad,
        grad_norm.reshape(1),
        new_first,
        new_second,
        new_master,
        new_master.astype(jnp.bfloat16),
        new_ema,
    )


def solution(mesh):
    placed = (
        P("dp", None),
        P("dp", None),
        P(None, None, "mp"),
        P("mp", None),
        P(None, "mp"),
        P("mp", None),
        P(),
        P(),
        P("dp"),
        P("dp"),
        P("dp"),
        P("dp"),
        P(),
        P("mp", "dp"),
        P("mp", "dp"),
        P("mp", "dp"),
        P("mp", "dp"),
    )
    return jax.shard_map(
        body,
        mesh=mesh,
        in_specs=placed,
        out_specs=(
            P("dp", None),
            P("dp", None),
            P(),
            P("mp", "dp"),
            P("mp", "dp"),
            P("mp", "dp"),
            P("mp", "dp"),
            P("mp", "dp"),
        ),
        check_vma=False,
    )
```

profile of v0, /device:TPU:0, one launch (start us, length us, event | category | flops | bytes accessed | tf_op | source)
XLA Modules:
  0.0 1090.6 jit_solution(3661359143004507559)
XLA Ops:
  11.7 3.6 fusion.32
  16.0 5.8 collective-permute-start
  21.8 4.1 collective-permute-start.1
  25.9 3.2 collective-permute-start.2
  36.5 2.3 collective-permute-done.3
  38.8 5.0 collective-permute-done.4
  52.8 21.0 %all-reduce.16.cloned.1.call-done = bf16[384,1024]{1,0:T(8,128)(2,1)} async-done(((bf16[384,1024]{1,0:T(8,128)(2,1)}), bf16[384,1024]{1,0:T(8,128)(2,1)}) %all-reduce.16.cloned.1.call-update) | async-done | bytes 786448 | tf_op jit(solution)/shard_map/psum | solution.py:116
  76.3 11.1 %multiply_convert_fusion.1 = (bf16[384,2048]{1,0:T(8,128)(2,1)}, f32[384,2048]{1,0:T(8,128)S(1)}, f32[384,2048]{1,0:T(8,128)S(1)}) fusion(bf16[1024,2048]{1,0:T(8,128)(2,1)} %param.21, bf16[384,1024]{1,0:T(8,128)(2,1)S(1)} %copy-done.4, bf16[384,1024]{1,0:T(8,128)(2,1)S(1)} %copy-done.3, f32[1024]{0:T(1024)S(1)} %bitcast.123, f32[384]{0:T(512)S(1)} %fusion.71, ...), kind=kOutput, calls=%fused_computation.13 | convolution fusion | flops 1664876544 | bytes 13642752 | tf_op jit(solution)/shard_map/dot_general | solution.py:123
  87.4 2.7 add_convert_fusion
  91.3 2.7 convolution_convert_fusion.1
  95.2 5.3 convolution_convert_fusion.2
  100.6 14.0 %all-reduce.18.cloned.1.call-done = bf16[384,1024]{1,0:T(8,128)(2,1)} async-done(((bf16[384,1024]{1,0:T(8,128)(2,1)}), bf16[384,1024]{1,0:T(8,128)(2,1)}) %all-reduce.18.cloned.1.call-update) | async-done | bytes 786448 | tf_op jit(solution)/shard_map/psum | solution.py:137
  114.6 2.5 fusion.28
  122.5 3.8 fusion.42
  126.4 6.9 multiply_reduce_fusion
  134.1 5.6 multiply_convert_fusion
  142.1 2.0 broadcast_select_fusion
  145.4 7.2 fusion.82
  156.1 5.3 collective-permute-start.8
  161.4 4.6 collective-permute-start.7
  168.9 7.3 collective-permute-start.6
  176.2 2.5 fusion.40
  181.2 2.4 fusion.45
  183.6 4.2 fusion.30
  188.5 7.2 fusion.53
  195.6 6.5 reshape.387
  202.2 6.3 reshape.388
  208.5 3.1 convolution_bitcast_fusion
  211.6 2.7 copy-done.6
  215.5 2.1 fusion.93
  217.6 2.8 reshape.386
  220.4 3.1 slice_add_fusion
  223.5 3.8 pad_maximum_fusion
  227.3 6.5 copy.64
  233.8 5.1 reshape.385
  247.7 657.2 %all-reduce.22.cloned.1.call-done = (f32[16,98304]{1,0:T(8,128)}, f32[16,32768]{1,0:T(8,128)}, f32[16,131072]{1,0:T(8,128)}, f32[16,131072]{1,0:T(8,128)}) async-done(((f32[16,98304]{1,0:T(8,128)}, f32[16,32768]{1,0:T(8,128)}, f32[16,131072]{1,0:T(8,128)}, f32[16,131072]{1,0:T(8,128)}), (f32[16,98304]{1,0:T(8,128)}, f32[16,32768]{1,0:T(8,128)}, f32[16,131072]{1,0:T(8,128)}, ...) | async-done | bytes 25165840
  904.9 3.6 dynamic-slice_dynamic-update-slice_fusion.2
  908.5 2.6 dynamic-slice_dynamic-update-slice_fusion.3
  911.1 4.0 dynamic-slice_dynamic-update-slice_fusion.1
  915.1 4.0 dynamic-slice_dynamic-update-slice_fusion
  919.1 93.4 %all-reduce.20.cloned.1.call-done = (f32[16,512]{1,0:T(8,128)}, f32[16,512]{1,0:T(8,128)}) async-done(((f32[16,512]{1,0:T(8,128)}, f32[16,512]{1,0:T(8,128)}), (f32[16,512]{1,0:T(8,128)}, f32[16,512]{1,0:T(8,128)})) %all-reduce.20.cloned.1.call-update) | async-done | bytes 65552
  1012.4 2.0 constant_dynamic-update-slice_fusion.1
  1014.5 1.9 constant_dynamic-update-slice_fusion
  1016.4 5.1 multiply_reduce_fusion.1
  1021.5 3.5 add_convert_fusion.1
  1024.9 39.6 %psum.39 = f32[]{:T(128)} all-reduce(f32[]{:T(128)} %multiply_reduce_fusion.1), channel_id=1, replica_groups=mesh['dp'=16,'mp'=2] {'dp','mp'}, use_global_device_ids=true, to_apply=%region_26.27 | all-reduce | flops 1 | bytes 8 | tf_op jit(solution)/shard_map/psum | solution.py:220
  1065.3 15.1 %multiply_add_fusion.1 = (f32[1,394240]{1,0:T(1,128)}, f32[1,394240]{1,0:T(1,128)S(1)}, f32[1,394240]{1,0:T(1,128)}, f32[1,394240]{1,0:T(1,128)}) fusion(f32[1,394240]{1,0:T(1,128)} %param.33, f32[1,394240]{1,0:T(1,128)} %param.30, f32[1,394240]{1,0:T(1,128)} %bitcast.41, f32[]{:T(128)} %bitcast.42, f32[1,394240]{1,0:T(1,128)} %constant_dynamic-update-slice_fusion, ...), kind=kLoop, calls=%fused_computation.55 | loop fusion | flops 7096320 | bytes 15769608 | tf_op jit(solution)/shard_map/add | solution.py:238
  1080.4 2.3 convert_element_type.164
  (219 shorter events, 51.9 us)
Async XLA Ops:
  7.2 43.9 %copy-start = (bf16[512,1024]{1,0:T(8,128)(2,1)S(1)}, bf16[512,1024]{1,0:T(8,128)(2,1)}, u32[]{:S(2)}) copy-start(bf16[512,1024]{1,0:T(8,128)(2,1)} %param.20) | copy-start | bytes 3145732
  7.2 3.2 copy-start.3
  7.2 66.6 %all-reduce.16.cloned.1.call-start = ((), (), s32[]{:S(2)}) async-start(), calls=%async_computation | async-start | bytes 1572864 | tf_op jit(solution)/shard_map/psum | solution.py:116
  9.1 67.2 %copy-start.37 = (f32[1,1024]{1,0:T(1,128)}, f32[1,1024]{1,0:T(1,128)S(1)}, u32[]{:S(2)}) copy-start(f32[1,1024]{1,0:T(1,128)S(1)} %get-tuple-element.100) | copy-start | bytes 12292
  11.7 3.6 copy-start.11
  16.0 15.7 %collective-permute-start = (bf16[2,96,512]{2,1,0:T(8,128)(2,1)}, bf16[2,96,512]{2,1,0:T(8,128)(2,1)S(1)}, u32[]{:S(2)}, u32[]{:S(2)}) collective-permute-start(bf16[2,96,512]{2,1,0:T(8,128)(2,1)} %slice.99), channel_id=1, source_target_pairs={{0,6},{2,8},{4,10},{6,12},{8,14},{10,16},{12,18},{14,20},{16,22},{... | collective-permute-start | bytes 589832 | tf_op jit(solution)/shard_map/ppermute | solution.py:26
  21.8 14.6 %collective-permute-start.1 = (bf16[2,96,512]{2,1,0:T(8,128)(2,1)}, bf16[2,96,512]{2,1,0:T(8,128)(2,1)}, u32[]{:S(2)}, u32[]{:S(2)}) collective-permute-start(bf16[2,96,512]{2,1,0:T(8,128)(2,1)} %slice.99), channel_id=1, source_target_pairs={{0,4},{2,6},{4,8},{6,10},{8,12},{10,14},{12,16},{14,18},{16,20},{1... | collective-permute-start | bytes 589832 | tf_op jit(solution)/shard_map/ppermute | solution.py:26
  25.9 10.5 collective-permute-start.2
  29.1 9.7 collective-permute-start.3
  30.4 13.3 %collective-permute-start.4 = (bf16[2,96,512]{2,1,0:T(8,128)(2,1)}, bf16[2,96,512]{2,1,0:T(8,128)(2,1)}, u32[]{:S(2)}, u32[]{:S(2)}) collective-permute-start(bf16[2,96,512]{2,1,0:T(8,128)(2,1)} %slice.99), channel_id=1, source_target_pairs={{4,0},{6,2},{8,4},{10,6},{12,8},{14,10},{16,12},{18,14},{20,16},{2... | collective-permute-start | bytes 589832 | tf_op jit(solution)/shard_map/ppermute | solution.py:26
  32.4 11.4 %collective-permute-start.5 = (bf16[2,96,512]{2,1,0:T(8,128)(2,1)}, bf16[2,96,512]{2,1,0:T(8,128)(2,1)}, u32[]{:S(2)}, u32[]{:S(2)}) collective-permute-start(bf16[2,96,512]{2,1,0:T(8,128)(2,1)} %slice.99), channel_id=1, source_target_pairs={{6,0},{8,2},{10,4},{12,6},{14,8},{16,10},{18,12},{20,14},{22,16},{... | collective-permute-start | bytes 589832 | tf_op jit(solution)/shard_map/ppermute | solution.py:26
  34.0 11.1 %copy-start.15 = (bf16[1,384,512]{1,2,0:T(8,128)(2,1)}, bf16[1,384,512]{1,2,0:T(8,128)(2,1)S(1)}, u32[]{:S(2)}) copy-start(bf16[1,384,512]{1,2,0:T(8,128)(2,1)S(1)} %copy.54) | copy-start | bytes 1179652
  34.9 11.7 %copy-start.13 = (bf16[1,384,512]{1,2,0:T(8,128)(2,1)}, bf16[1,384,512]{1,2,0:T(8,128)(2,1)S(1)}, u32[]{:S(2)}) copy-start(bf16[1,384,512]{1,2,0:T(8,128)(2,1)S(1)} %copy.55) | copy-start | bytes 1179652
  36.4 11.0 %copy-start.21 = (bf16[1,384,512]{1,2,0:T(8,128)(2,1)}, bf16[1,384,512]{1,2,0:T(8,128)(2,1)S(1)}, u32[]{:S(2)}) copy-start(bf16[1,384,512]{1,2,0:T(8,128)(2,1)S(1)} %copy.52) | copy-start | bytes 1179652
  52.6 62.0 %all-reduce.18.cloned.1.call-start = ((), (), s32[]{:S(2)}) async-start(), calls=%async_computation.1 | async-start | bytes 1572864 | tf_op jit(solution)/shard_map/psum | solution.py:137
  52.8 34.6 %copy-start.48 = (f32[384]{0:T(512)}, f32[384]{0:T(512)S(1)}, u32[]{:S(2)}) copy-start(f32[384]{0:T(512)S(1)} %fusion.68) | copy-start | bytes 4612
  75.3 12.1 %copy-start.39 = (f32[384]{0:T(512)}, f32[384]{0:T(512)S(1)}, u32[]{:S(2)}) copy-start(f32[384]{0:T(512)S(1)} %broadcast_multiply_fusion) | copy-start | bytes 4612
  75.8 11.6 %copy-start.44 = (f32[384]{0:T(512)}, f32[384]{0:T(512)S(1)}, u32[]{:S(2)}) copy-start(f32[384]{0:T(512)S(1)} %fusion.71) | copy-start | bytes 4612
  76.3 11.1 %copy-start.8 = (bf16[384,1024]{1,0:T(8,128)(2,1)S(1)}, bf16[384,1024]{1,0:T(8,128)(2,1)}, u32[]{:S(2)}) copy-start(bf16[384,1024]{1,0:T(8,128)(2,1)} %param.18) | copy-start | bytes 2359300
  76.3 11.1 %copy-start.62 = (bf16[2048,1024]{1,0:T(8,128)(2,1)S(1)}, bf16[2048,1024]{1,0:T(8,128)(2,1)}, u32[]{:S(2)}) copy-start(bf16[2048,1024]{1,0:T(8,128)(2,1)} %param.22) | copy-start | bytes 12582916
  87.4 3.9 copy-start.61
  94.1 150.2 %all-reduce.24.cloned.1.call-start = ((), (), s32[]{:S(2)}) async-start(), calls=%async_computation.4 | async-start | bytes 3145728 | tf_op jit(solution)/shard_map/psum | solution.py:126
  122.5 3.9 copy-start.22
  122.5 3.9 copy-start.29
  134.1 5.6 copy-start.16
  141.2 4.2 copy-start.38
  141.2 4.2 copy-start.41
  141.2 4.2 copy-start.46
  144.1 24.8 %collective-permute-start.11 = (bf16[2,96,512]{2,1,0:T(8,128)(2,1)}, bf16[2,96,512]{2,1,0:T(8,128)(2,1)}, u32[]{:S(2)}, u32[]{:S(2)}) collective-permute-start(bf16[2,96,512]{2,1,0:T(8,128)(2,1)} %get-tuple-element.92), channel_id=1, source_target_pairs={{6,0},{8,2},{10,4},{12,6},{14,8},{16,10},{18,12},{20,14},{22,16},{... | collective-permute-start | bytes 589832 | tf_op jit(solution)/shard_map/ppermute | solution.py:26
  152.6 23.6 %copy-start.14 = (bf16[1,384,512]{1,2,0:T(8,128)(2,1)S(1)}, bf16[1,384,512]{1,2,0:T(8,128)(2,1)}, u32[]{:S(2)}) copy-start(bf16[1,384,512]{1,2,0:T(8,128)(2,1)} %copy-done.13) | copy-start | bytes 1179652
  153.4 14.5 %slice-start.1 = ((bf16[480,8,64]{0,2,1:T(8,128)(2,1)}), bf16[384,8,64]{0,2,1:T(8,128)(2,1)S(1)}, s32[]{:S(2)}) async-start(bf16[480,8,64]{0,2,1:T(8,128)(2,1)} %copy-done.20), calls=%async_computation.6 | async-start | bytes 786432 | tf_op jit(solution)/shard_map/slice | solution.py:180
  153.4 15.5 %copy-start.33 = (bf16[2,96,512]{2,1,0:T(8,128)(2,1)S(1)}, bf16[2,96,512]{2,1,0:T(8,128)(2,1)}, u32[]{:S(2)}) copy-start(bf16[2,96,512]{2,1,0:T(8,128)(2,1)} %get-tuple-element.87) | copy-start | bytes 589828
  153.4 26.2 %collective-permute-start.10 = (bf16[2,96,512]{2,1,0:T(8,128)(2,1)}, bf16[2,96,512]{2,1,0:T(8,128)(2,1)}, u32[]{:S(2)}, u32[]{:S(2)}) collective-permute-start(bf16[2,96,512]{2,1,0:T(8,128)(2,1)} %get-tuple-element.91), channel_id=1, source_target_pairs={{4,0},{6,2},{8,4},{10,6},{12,8},{14,10},{16,12},{18,14},{20,16},{2... | collective-permute-start | bytes 589832 | tf_op jit(solution)/shard_map/ppermute | solution.py:26
  154.8 24.8 %collective-permute-start.9 = (bf16[2,96,512]{2,1,0:T(8,128)(2,1)}, bf16[2,96,512]{2,1,0:T(8,128)(2,1)}, u32[]{:S(2)}, u32[]{:S(2)}) collective-permute-start(bf16[2,96,512]{2,1,0:T(8,128)(2,1)} %get-tuple-element.90), channel_id=1, source_target_pairs={{2,0},{4,2},{6,4},{8,6},{10,8},{12,10},{14,12},{16,14},{18,16},{20... | collective-permute-start | bytes 589832 | tf_op jit(solution)/shard_map/ppermute | solution.py:26
  156.1 23.5 %collective-permute-start.8 = (bf16[2,96,512]{2,1,0:T(8,128)(2,1)}, bf16[2,96,512]{2,1,0:T(8,128)(2,1)}, u32[]{:S(2)}, u32[]{:S(2)}) collective-permute-start(bf16[2,96,512]{2,1,0:T(8,128)(2,1)} %get-tuple-element.89), channel_id=1, source_target_pairs={{0,2},{2,4},{4,6},{6,8},{8,10},{10,12},{12,14},{14,16},{16,18},{18... | collective-permute-start | bytes 589832 | tf_op jit(solution)/shard_map/ppermute | solution.py:26
  161.4 18.2 %collective-permute-start.7 = (bf16[2,96,512]{2,1,0:T(8,128)(2,1)}, bf16[2,96,512]{2,1,0:T(8,128)(2,1)}, u32[]{:S(2)}, u32[]{:S(2)}) collective-permute-start(bf16[2,96,512]{2,1,0:T(8,128)(2,1)} %get-tuple-element.88), channel_id=1, source_target_pairs={{0,4},{2,6},{4,8},{6,10},{8,12},{10,14},{12,16},{14,18},{16,20},{1... | collective-permute-start | bytes 589832 | tf_op jit(solution)/shard_map/ppermute | solution.py:26
  168.9 10.8 collective-permute-start.6
  187.8 717.1 %all-reduce.22.cloned.1.call-start = ((), (), s32[]{:S(2)}) async-start(), calls=%async_computation.3 | async-start | bytes 50331648
  202.1 6.3 copy-start.12
  220.4 3.1 slice-start
  238.9 5.3 copy-start.36
  238.9 5.3 copy-start.43
  238.9 773.5 %all-reduce.20.cloned.1.call-start = ((), (), s32[]{:S(2)}) async-start(), calls=%async_computation.2 | async-start | bytes 131072
  240.5 5.5 copy-start.60
  240.5 5.5 copy-start.56
  240.5 5.5 copy-start.52
  915.1 106.4 %copy-start.54 = (f32[384]{0:T(512)S(1)}, f32[384]{0:T(512)}, u32[]{:S(2)}) copy-start(f32[384]{0:T(512)} %copy-done.53) | copy-start | bytes 4612
  1012.4 9.0 copy-start.27
  (35 other events, 59.2 us)
Sparse Core Ops, SparseCore 0:
  52.7 21.1 all-reduce.15
  94.2 20.3 all-reduce.17
  188.0 21.7 all-reduce.23
  239.0 665.8 all-reduce.21
  910.9 101.4 all-reduce.19
where the time goes:
time: 1100 us; the launch traced here: 1090 us
  waiting for transfers between devices  793 us (72%)
  matrix products  74.7 us (7%)
  local copies, waits for them, and re-layouts  71.7 us (7%)
  other arithmetic  52.2 us (5%)
  blocking collectives  39.6 us (4%)
  starting transfers between devices  39.1 us (4%)
  between operations  20.3 us (2%)
    unnamed x7, waiting for transfers between devices  751 us
    psum x1, blocking collectives, body(): square_sum = lax.psum(jnp.sum(gradient * gradient), ('dp', 'mp'))  39.6 us
    ppermute x12, starting transfers between devices, passed_along(): lax.ppermute(value, axis, [(source, source + steps) for source in range(l...  38.1 us
    unnamed x138, local copies, waits for them, and re-layouts  32.8 us
  transfers between devices with their start and end apart: 17, of which 6 were waited for; matrix products, arithmetic and copies ran while one was open for 8% of the time, Pallas kernels for 0%

commit v1 on v0

v1 whole, which is shorter than its diff:
```python
import functools

import jax
import jax.numpy as jnp
from jax import lax
from jax.experimental import pallas as pl
from jax.experimental.pallas import tpu as pltpu
from jax.sharding import PartitionSpec as P

D = 1024
HDIM = 64
FF = 4096
SECTIONS = 8
TOK = 384
PMAX = 96
KEYS = TOK + PMAX
OUT_FAN = 2
HW = D // 2
HF = FF // 2
HEADS = HW // HDIM
CLIP_NORM = 1.0
BETA_ONE = 0.5
BETA_TWO = 0.5
WEIGHT_DECAY = 0.1
EMA_DECAY = 0.75

BF = jnp.bfloat16
F32 = jnp.float32
MP, PX, PY, PLANE, OUTER, LENGTH, SOURCE, PROMPT, SECTION = range(9)


def shaped(shape, dtype):
    return jax.ShapeDtypeStruct(shape, dtype)


def dot_nn(a, b):
    return lax.dot_general(a, b, (((1,), (0,)), ((), ())), preferred_element_type=F32)


def dot_nt(a, b):
    return lax.dot_general(a, b, (((1,), (1,)), ((), ())), preferred_element_type=F32)


def dot_tn(a, b):
    return lax.dot_general(a, b, (((0,), (0,)), ((), ())), preferred_element_type=F32)


def block(shape, index):
    return pl.BlockSpec(shape, index)


def whole(shape):
    rank = len(shape)
    return pl.BlockSpec(shape, lambda *_: (0,) * rank)


def call(kernel, meta, inputs, in_specs, outs, out_specs, grid=(1,), scratch=(), flops=0, name=None, vmem=30):
    moved = sum(a.size * a.dtype.itemsize for a in list(inputs) + list(outs))
    return pl.pallas_call(
        kernel,
        grid_spec=pltpu.PrefetchScalarGridSpec(
            num_scalar_prefetch=1, grid=grid, in_specs=in_specs, out_specs=out_specs, scratch_shapes=scratch
        ),
        out_shape=outs,
        compiler_params=pltpu.CompilerParams(vmem_limit_bytes=vmem << 20),
        cost_estimate=pl.CostEstimate(flops=int(flops), bytes_accessed=int(moved), transcendentals=0),
        name=name,
    )(meta, *inputs)


def simple(kernel, meta, inputs, outs, **kw):
    return call(kernel, meta, inputs, [whole(a.shape) for a in inputs], outs, [whole(o.shape) for o in outs], **kw)


def unit_rows(values):
    centred = values - jnp.mean(values, axis=-1, keepdims=True)
    scale = lax.rsqrt(jnp.mean(centred * centred, axis=-1, keepdims=True) + 1e-05)
    return centred * scale, scale


def norm_back(grad, gain_row, unit, scale):
    e = gain_row * grad
    return scale * (e - jnp.mean(e, axis=-1, keepdims=True) - unit * jnp.mean(e * unit, axis=-1, keepdims=True))


def row_of(ref, which, meta):
    return ref[which, pl.ds(meta[SECTION], 1), :]


def valid_rows(meta):
    return lax.broadcasted_iota(jnp.int32, (TOK, 1), 0) < meta[LENGTH]


def keys_ok(meta):
    at = lax.broadcasted_iota(jnp.int32, (KEYS, 1), 0)
    return at < jnp.where(at < TOK, meta[LENGTH], TOK + meta[PROMPT])


def prompt_norm_kernel(meta, tokens, gain, shift, out):
    unit, _ = unit_rows(tokens[...].astype(F32))
    out[...] = (row_of(gain, 0, meta) * unit + row_of(shift, 0, meta)).astype(BF)


def mask_kernel(meta, cotangent, low, half):
    kept = jnp.where(valid_rows(meta), cotangent[...], jnp.zeros((), BF))
    low[...] = kept

    @pl.when(meta[MP] == 0)
    def _():
        half[...] = kept[:, :HW]

    @pl.when(meta[MP] == 1)
    def _():
        half[...] = kept[:, HW:]


def qkv_kernel(meta, tokens, gain, shift, weight, normed, projected):
    @pl.when(pl.program_id(0) == 0)
    def _():
        unit, _ = unit_rows(tokens[...].astype(F32))
        normed[...] = (row_of(gain, 0, meta) * unit + row_of(shift, 0, meta)).astype(BF)

    projected[0] = dot_nn(normed[...], weight[0]).astype(BF)


def grad_act_kernel(meta, low, down, out):
    out[...] = dot_nt(low[...], down[...])


def attend_kernel(meta, projected, here, there, qkv, out_weight, normed_prompt, prompt_pair, attended_t, log_total, partial, keys, values, values_t):
    half = PMAX // 2
    normed_prompt[pl.ds(pl.multiple_of(meta[MP] * half, half), half), :] = here[...]
    normed_prompt[pl.ds(pl.multiple_of((1 - meta[MP]) * half, half), half), :] = there[...]
    rows = normed_prompt[...]
    pair_k = dot_nn(rows, qkv[1]).astype(BF)
    pair_v = dot_nn(rows, qkv[2]).astype(BF)
    prompt_pair[0] = pair_k
    prompt_pair[1] = pair_v
    keys[:TOK] = projected[1]
    keys[TOK:] = pair_k
    values[:TOK] = projected[2]
    values[TOK:] = pair_v
    values_t[...] = values[...].T
    counted = keys_ok(meta)
    lane = lax.broadcasted_iota(jnp.int32, (1, 2 * HDIM), 1)
    for head in range(HEADS):
        at = (head // 2) * 2 * HDIM
        mine = jnp.where((lane // HDIM) == head % 2, HDIM ** (-0.5), 0.0).astype(BF)
        query = projected[0, :, at : at + 2 * HDIM] * mine
        scores = jnp.where(counted, dot_nt(keys[:, at : at + 2 * HDIM], query), -1e30)
        top = jnp.max(scores, axis=0, keepdims=True)
        grown = jnp.exp(scores - top)
        total = jnp.sum(grown, axis=0, keepdims=True)
        probability = (grown * (1.0 / total)).astype(BF)
        rows_at = slice(head * HDIM, (head + 1) * HDIM)
        attended_t[rows_at, :] = dot_nn(values_t[rows_at, :], probability).astype(BF)
        log_total[head : head + 1, :] = top + jnp.log(total)
    partial[...] = dot_tn(attended_t[...], out_weight[...]).astype(BF)


TILE = 256


def ffn_kernel(split, meta, tokens, here, there, gain, shift, up, grad_act, hidden, normed, act, pre_low, partial, total):
    step = pl.program_id(0)

    @pl.when(step == 0)
    def _():
        state = tokens[...].astype(F32) + (here[...].astype(F32) + there[...].astype(F32))
        hidden[...] = state
        unit, _ = unit_rows(state)
        normed[...] = (row_of(gain, 1, meta) * unit + row_of(shift, 1, meta)).astype(BF)
        total[...] = jnp.zeros_like(total)

    pre = dot_nn(normed[...], up[...])
    cdf = 0.5 * (1.0 + lax.erf(pre * (0.5**0.5)))
    slope = cdf + pre * (jnp.exp(-0.5 * pre * pre) * (0.5 / jnp.pi) ** 0.5)
    activated = (pre * cdf).astype(BF)
    grad = (grad_act[...] * slope).astype(BF)
    pre_low[...] = grad
    if split:
        for sub in range(TILE // split):
            number = step * (TILE // split) + sub
            piece = jnp.bitwise_xor(lax.rem(number, 4), meta[PLANE])
            at = pl.multiple_of((number // 4) * split, split)
            act[piece, :, pl.ds(at, split)] = activated[:, sub * split : (sub + 1) * split]
    else:
        act[0, :, pl.ds(pl.multiple_of(step * TILE, TILE), TILE)] = activated
    total[...] += dot_nt(grad, up[...])

    @pl.when(step == pl.num_programs(0) - 1)
    def _():
        partial[...] = total[...].astype(BF)


def down_kernel(split, meta, act, down, partial, total):
    step = pl.program_id(0)

    @pl.when(step == 0)
    def _():
        total[...] = jnp.zeros_like(total)

    if split:
        for sub in range(TILE // split):
            number = step * (TILE // split) + sub
            piece = jnp.bitwise_xor(lax.rem(number, 4), meta[PLANE])
            at = pl.multiple_of((number // 4) * split, split)
            total[...] += dot_nn(act[piece, :, pl.ds(at, split)], down[sub * split : (sub + 1) * split, :])
    else:
        total[...] += dot_nn(act[0, :, pl.ds(pl.multiple_of(step * TILE, TILE), TILE)], down[...])

    @pl.when(step == pl.num_programs(0) - 1)
    def _():
        partial[...] = total[...].astype(BF)


def block_out_kernel(meta, hidden, here, there, out):
    out[...] = (hidden[...] + (here[...].astype(F32) + there[...].astype(F32))).astype(BF)


def attend_back_kernel(
    meta, here, there, hidden, gain, low, out_weight, projected, prompt_pair, log_total,
    local, sent, grad_hidden, hidden_low, tables, keys, values, keys_t, grads, query_t,
):
    back = here[...].astype(F32) + there[...].astype(F32)
    unit, scale = unit_rows(hidden[...])
    full = low[...].astype(F32) + norm_back(back, row_of(gain, 1, meta), unit, scale)
    grad_hidden[...] = full
    tables[0:1, :] = jnp.sum(back * unit, axis=0, keepdims=True)
    tables[1:2, :] = jnp.sum(back, axis=0, keepdims=True)
    rounded = full.astype(BF)
    hidden_low[...] = rounded
    grads[...] = dot_nt(rounded, out_weight[...]).astype(BF)
    keys[:TOK] = projected[1]
    keys[TOK:] = prompt_pair[0]
    values[:TOK] = projected[2]
    values[TOK:] = prompt_pair[1]
    keys_t[...] = keys[...].T
    counted = keys_ok(meta)
    lane = lax.broadcasted_iota(jnp.int32, (1, 2 * HDIM), 1)
    left = lane < HDIM
    for pair in range(HEADS // 2):
        at = pair * 2 * HDIM
        span = slice(at, at + 2 * HDIM)
        key_pair, value_pair = keys[:, span], values[:, span]
        query_pair = projected[0, :, span] * jnp.asarray(HDIM ** (-0.5), BF)
        grad_pair = grads[:, span]
        found = []
        for head in (2 * pair, 2 * pair + 1):
            mine = ((lane // HDIM) == head % 2).astype(BF)
            scores = jnp.where(counted, dot_nt(key_pair, query_pair * mine), -1e30)
            probability = jnp.exp(scores - log_total[head : head + 1, :])
            grad_prob = dot_nt(value_pair, grad_pair * mine)
            centre = jnp.sum(probability * grad_prob, axis=0, keepdims=True)
            grad_scores = (probability * (grad_prob - centre)).astype(BF)
            rows_at = slice(head * HDIM, (head + 1) * HDIM)
            query_t[rows_at, :] = dot_nn(keys_t[rows_at, :], grad_scores) * HDIM ** (-0.5)
            found.append((dot_nn(grad_scores, query_pair), dot_nn(probability.astype(BF), grad_pair)))
        local[1, :, span] = jnp.where(left, found[0][0], found[1][0]).astype(BF)
        local[2, :, span] = jnp.where(left, found[0][1], found[1][1]).astype(BF)
    local[0, :TOK, :] = query_t[...].T.astype(BF)
    local[0, TOK:, :] = jnp.zeros((PMAX, HW), BF)
    relative = jnp.bitwise_xor(lax.rem(meta[SOURCE], 4), meta[PLANE])
    for k in range(1, 4):
        keep = relative == k
        for c in range(2):
            sent[k - 1, c] = jnp.where(keep, local[1 + c, TOK:, :], jnp.zeros((), BF))


def grad_normed_kernel(meta, local, first, second, third, qkv, out, returned_low, total):
    c = pl.program_id(0)

    @pl.when(c == 0)
    def _():
        total[...] = jnp.zeros_like(total)

    total[...] += dot_nt(local[0, :TOK, :], qkv[0])

    @pl.when(c > 0)
    def _():
        at = c - 1
        returned = first[at].astype(F32) + second[at].astype(F32) + third[at].astype(F32)
        returned_low[...] = returned.astype(BF)
        total[:PMAX, :] += dot_nt(returned_low[...], qkv[0])

    @pl.when(c == 2)
    def _():
        out[...] = total[...].astype(BF)


def input_grad_kernel(meta, here, there, tokens, gain, grad_hidden, out, tables):
    back = here[...].astype(F32) + there[...].astype(F32)
    unit, scale = unit_rows(tokens[...].astype(F32))
    out[...] = (grad_hidden[...] + norm_back(back, row_of(gain, 0, meta), unit, scale)).astype(BF)
    tables[0:1, :] = jnp.sum(back * unit, axis=0, keepdims=True)
    tables[1:2, :] = jnp.sum(back, axis=0, keepdims=True)


def part_out(out, at, whole_ref, axis, side):
    if axis == "x":
        out[..., at] = whole_ref[:, :, side]
    else:
        out[..., at] = whole_ref[:, side]


def up_product_kernel(axis, meta, normed, pre_low, away, kept, held):
    held[...] = dot_tn(normed[...], pre_low[...]).astype(BF).reshape(held.shape)
    side = meta[PX] if axis == "x" else meta[PY]
    if axis == "x":
        away[...] = held[:, :, 1 - side]
        kept[...] = held[:, :, side]
    else:
        away[...] = held[:, 1 - side]
        kept[...] = held[:, side]


def down_product_kernel(meta, mine, act_a, act_b, act_c, low, low_a, low_b, low_c, swap_a, swap_b, swap_c, own, away, lows, held):
    @pl.when(pl.program_id(0) == 0)
    def _():
        here = pl.multiple_of(meta[MP] * HW, HW)
        there = pl.multiple_of((1 - meta[MP]) * HW, HW)
        for k, (half, other) in enumerate(((low_a, swap_a), (low_b, swap_b), (low_c, swap_c))):
            lows[k, :, pl.ds(here, HW)] = half[...]
            lows[k, :, pl.ds(there, HW)] = other[...]

    at = pl.ds(pl.multiple_of(pl.program_id(0) * TILE, TILE), TILE)
    found = dot_tn(mine[...], low[:, at])
    for k, act in enumerate((act_a, act_b, act_c)):
        found += dot_tn(act[...], lows[k, :, at])
    held[...] = found.reshape(held.shape)
    own[...] = held[meta[OUTER]]
    for m in range(1, held.shape[0]):
        away[m - 1] = held[jnp.bitwise_xor(meta[OUTER], m)].astype(BF)


def qkv_product_kernel(axis, meta, normed, normed_prompt, local, away, kept, normed_t, held):
    c = pl.program_id(0)

    @pl.when(c == 0)
    def _():
        normed_t[:, :TOK] = normed[...].T
        normed_t[:, TOK:] = normed_prompt[...].T

    held[pl.ds(pl.multiple_of(c * D, D), D), :] = dot_nn(normed_t[...], local[0]).astype(BF)

    @pl.when(c == 2)
    def _():
        outer, _, rows, columns = away.shape
        parts = held[...].reshape(outer, 2, 2, rows, columns)
        if axis == "x":
            low_side, high_side = parts[:, :, 0], parts[:, :, 1]
            side = meta[PX]
        else:
            low_side, high_side = parts[:, 0], parts[:, 1]
            side = meta[PY]
        away[...] = jnp.where(side == 0, high_side, low_side)
        kept[...] = jnp.where(side == 0, low_side, high_side)


def out_product_kernel(meta, attended_t, hidden_low, tables, away_x, kept_x, away_y, kept_y, held_x, held_y):
    found = dot_nn(attended_t[...], hidden_low[...]).astype(BF)
    rows = held_x.shape[3]
    held_x[..., :HW] = found[:, :HW].reshape(held_x.shape[:3] + (rows, HW))
    held_x[..., HW:] = tables[...].reshape(held_x.shape[:3] + (rows, 128))
    held_y[...] = found[:, HW:].reshape(held_y.shape)
    away_x[...] = held_x[:, :, 1 - meta[PX]]
    kept_x[...] = held_x[:, :, meta[PX]]
    away_y[...] = held_y[:, 1 - meta[PY]]
    kept_y[...] = held_y[:, meta[PY]]


def second_kernel(meta, kept_x, got_x, kept_y, got_y, away_x, own_x, away_y, own_y, held_x, held_y):
    held_x[...] = kept_x[...].astype(F32) + got_x[...].astype(F32)
    held_y[...] = kept_y[...].astype(F32) + got_y[...].astype(F32)
    away_x[...] = held_x[:, 1 - meta[PY]].astype(BF)
    own_x[...] = held_x[:, meta[PY]].astype(BF)
    away_y[...] = held_y[:, 1 - meta[PX]].astype(BF)
    own_y[...] = held_y[:, meta[PX]].astype(BF)


def third_kernel(radix, meta, kept_x, got_x, kept_y, got_y, own, away, held):
    left = kept_x.shape[-1]
    held[..., :left] = kept_x[...].astype(F32) + got_x[...].astype(F32)
    held[..., left:] = kept_y[...].astype(F32) + got_y[...].astype(F32)
    rest = held.shape[0] // radix
    digit = meta[OUTER] // rest
    for m in range(radix):
        at = pl.ds(jnp.bitwise_xor(digit, m) * rest, rest)
        if m == 0:
            own[...] = held[at]
        else:
            away[m - 1] = held[at].astype(BF)


def to_rows(out, at, value):
    rows, columns = value.shape
    across = columns // 128
    for j in range(across):
        piece = value[:, 128 * j : 128 * (j + 1)]
        if across == 1:
            out[at : at + rows, :] = piece
        else:
            out[pl.ds(at + j, rows, stride=across), :] = piece


def finish_kernel(received, meta, *refs):
    *ins, out, squares = refs
    sums = []
    for k in range(4):
        own, got = ins[2 * k], ins[2 * k + 1]
        value = own[0]
        for m in range(received):
            value = value + got[m, 0].astype(F32)
        sums.append(value)
    at = 0
    tables = sums[1][:, HW : HW + 128]
    third = jnp.concatenate([sums[1][:, :HW], sums[1][:, HW + 128 :]], axis=1)
    for value in (sums[0], third, sums[2], sums[3]):
        to_rows(out, at, value)
        at += value.size // 128
    entries = out.shape[0] - at
    out[at:, :] = tables[:entries, :]
    total = jnp.sum(tables * tables, axis=0, keepdims=True)
    for value in (sums[0], third, sums[2], sums[3]):
        line = jnp.sum(value * value, axis=0, keepdims=True)
        for j in range(value.shape[1] // 128):
            total = total + line[:, 128 * j : 128 * (j + 1)]
    squares[...] = jnp.broadcast_to(jnp.sum(total, axis=1, keepdims=True), squares.shape)


def adam_kernel(bounds, rates, meta, square_sum, fixes, gradient, master, first, second, ema, new_first, new_second, new_master, copy, new_ema):
    norm = jnp.sqrt(square_sum[0:1, 0:1])
    clip = jnp.minimum(1.0, CLIP_NORM / (norm + 1e-06))
    rows = gradient.shape[0]
    at = pl.program_id(0) * rows + lax.broadcasted_iota(jnp.int32, (rows, 1), 0)
    rate = jnp.full((rows, 1), rates[0], F32)
    for bound, value in zip(bounds, rates[1:]):
        rate = jnp.where(at >= bound, value, rate)
    clipped = clip * gradient[...]
    moment = BETA_ONE * first[...] + (1.0 - BETA_ONE) * clipped
    square = BETA_TWO * second[...] + (1.0 - BETA_TWO) * clipped * clipped
    new_first[...] = moment
    new_second[...] = square
    one, two = fixes[0:1, 0:1], fixes[0:1, 1:2]
    update = (moment * one) / (jnp.sqrt(square * two) + 1e-08)
    weights = master[...] - rate * (update + WEIGHT_DECAY * master[...])
    new_master[...] = weights
    copy[...] = weights.astype(BF)
    new_ema[...] = EMA_DECAY * ema[...] + (1.0 - EMA_DECAY) * weights


def partner(value, axis, flip):
    count = lax.axis_size(axis)
    return lax.ppermute(value, axis, [(i, i ^ flip) for i in range(count)])


def radices(outer):
    found = []
    while outer > 1:
        step = 4 if outer % 4 == 0 else 2
        found.append(step)
        outer //= step
    return found


def outer_steps(own, away, outer, outer_index):
    steps = radices(outer)
    rest = outer // steps[0]
    got = [partner(away[m - 1], "dp", 4 * m * rest) for m in range(1, steps[0])]
    for radix in steps[1:]:
        total = own
        for item in got:
            total = total + item.astype(F32)
        width = rest
        rest //= radix
        digit = lax.rem(outer_index, width) // rest
        cut = total.reshape((radix, rest) + total.shape[1:])
        own = lax.dynamic_index_in_dim(cut, digit, 0, keepdims=False)
        got = [
            partner(lax.dynamic_index_in_dim(cut, digit ^ m, 0, keepdims=False).astype(BF), "dp", 4 * m * rest)
            for m in range(1, radix)
        ]
    return own, got


def body(
    tokens, cotangent, qkv_weight, out_weight, up_weight, down_weight, norm_gain, norm_shift,
    lengths, prompt_src, prompt_len, codebook_section, adam_step, master, first_moment, second_moment, ema_weight,
):
    dp_index = lax.axis_index("dp")
    mp_index = lax.axis_index("mp")
    count = lax.axis_size("dp")
    outer = count // 4
    plane, outer_index = lax.rem(dp_index, 4), dp_index // 4
    meta = jnp.stack(
        [mp_index, plane % 2, plane // 2, plane, outer_index, lengths[0], prompt_src[0], prompt_len[0], codebook_section[0]]
    ).astype(jnp.int32)
    first_radix = radices(outer)[0]
    rest = outer // first_radix

    half_rows = PMAX // 2
    (prompt_rows,) = call(
        prompt_norm_kernel, meta, (tokens, norm_gain, norm_shift),
        [block((half_rows, D), lambda i, m: (m[MP], 0)), whole(norm_gain.shape), whole(norm_shift.shape)],
        [shaped((half_rows, D), BF)], [whole((half_rows, D))], name="prompt_norm",
    )
    rows_from = [partner(prompt_rows, "dp", k) for k in (1, 2, 3)]
    low, low_half = simple(
        mask_kernel, meta, (cotangent,), [shaped((TOK, D), BF), shaped((TOK, HW), BF)], name="mask"
    )
    hidden_rows = HF // count
    split = hidden_rows if hidden_rows % 128 == 0 else 0
    low_from = [partner(low_half, "dp", k) for k in (1, 2, 3)]
    low_swap = [partner(item, "mp", 1) for item in low_from]

    normed, projected = call(
        qkv_kernel, meta, (tokens, norm_gain, norm_shift, qkv_weight),
        [whole(tokens.shape), whole(norm_gain.shape), whole(norm_shift.shape), block((1, D, HW), lambda c, m: (c, 0, 0))],
        [shaped((TOK, D), BF), shaped((3, TOK, HW), BF)],
        [whole((TOK, D)), block((1, TOK, HW), lambda c, m: (c, 0, 0))],
        grid=(3,), flops=2 * TOK * D * 3 * HW, name="qkv",
    )
    (grad_act,) = call(
        grad_act_kernel, meta, (low, down_weight),
        [whole((TOK, D)), block((2 * TILE, D), lambda t, m: (t, 0))],
        [shaped((TOK, HF), F32)], [block((TOK, 2 * TILE), lambda t, m: (0, t))],
        grid=(HF // (2 * TILE),), flops=2 * TOK * D * HF, name="grad_act",
    )
    relative = jnp.bitwise_xor(lax.rem(prompt_src[0], 4), plane)
    here = jnp.where(relative == 1, rows_from[0], jnp.where(relative == 2, rows_from[1], rows_from[2]))
    there = partner(here, "mp", 1)
    normed_prompt, prompt_pair, attended_t, log_total, mixed = simple(
        attend_kernel, meta, (projected, here, there, qkv_weight, out_weight),
        [shaped((PMAX, D), BF), shaped((2, PMAX, HW), BF), shaped((HW, TOK), BF), shaped((HEADS, TOK), F32), shaped((TOK, D), BF)],
        scratch=[pltpu.VMEM((KEYS, HW), BF), pltpu.VMEM((KEYS, HW), BF), pltpu.VMEM((HW, KEYS), BF)],
        flops=2 * TOK * HW * (4 * KEYS + D), name="attend",
    )
    mixed_there = partner(mixed, "mp", 1)
    pieces = 4 if split else 1
    hidden, normed_second, act, pre_low, second_part = call(
        functools.partial(ffn_kernel, split), meta, (tokens, mixed, mixed_there, norm_gain, norm_shift, up_weight, grad_act),
        [whole((TOK, D))] * 3 + [whole(norm_gain.shape)] * 2
        + [block((D, TILE), lambda t, m: (0, t)), block((TOK, TILE), lambda t, m: (0, t))],
        [shaped((TOK, D), F32), shaped((TOK, D), BF), shaped((pieces, TOK, HF // pieces), BF), shaped((TOK, HF), BF), shaped((TOK, D), BF)],
        [whole((TOK, D)), whole((TOK, D)), whole((pieces, TOK, HF // pieces)), block((TOK, TILE), lambda t, m: (0, t)), whole((TOK, D))],
        grid=(HF // TILE,), scratch=[pltpu.VMEM((TOK, D), F32)], flops=4 * TOK * D * HF, name="ffn",
    )
    second_there = partner(second_part, "mp", 1)

    if split:
        act_pieces = [act[k] for k in range(4)]
    else:
        cut = act[0].reshape(TOK, outer, 4, hidden_rows)
        act_pieces = [
            lax.dynamic_index_in_dim(cut, plane ^ k, 2, keepdims=False).reshape(TOK, HF // 4) for k in range(4)
        ]
    act_from = [partner(act_pieces[k], "dp", k) for k in (1, 2, 3)]

    up_rows = D // count
    up_half = [shaped((outer, 2, up_rows, D), BF)] * 2

    def up_product(axis, at):
        return call(
            functools.partial(up_product_kernel, axis), meta, (normed_second, pre_low),
            [whole((TOK, D)), block((TOK, TILE), lambda t, m: (0, at + t))],
            up_half, [block((outer, 2, up_rows, TILE), lambda t, m: (0, 0, 0, t))] * 2,
            grid=(D // TILE,), scratch=[pltpu.VMEM((outer, 2, 2, up_rows, TILE), BF)],
            flops=2 * TOK * D * D, name="up_product_" + axis,
        )

    up_away_x, up_kept_x = up_product("x", 0)
    up_got_x = partner(up_away_x, "dp", 1)
    up_away_y, up_kept_y = up_product("y", D // TILE)
    up_got_y = partner(up_away_y, "dp", 2)

    local, sent, grad_hidden, hidden_low, tables_second = simple(
        attend_back_kernel, meta,
        (second_part, second_there, hidden, norm_gain, low, out_weight, projected, prompt_pair, log_total),
        [shaped((3, KEYS, HW), BF), shaped((3, 2, PMAX, HW), BF), shaped((TOK, D), F32), shaped((TOK, D), BF), shaped((2, D), F32)],
        scratch=[pltpu.VMEM((KEYS, HW), BF), pltpu.VMEM((KEYS, HW), BF), pltpu.VMEM((HW, KEYS), BF), pltpu.VMEM((TOK, HW), BF), pltpu.VMEM((HW, TOK), F32)],
        flops=2 * TOK * HW * (10 * KEYS + D), name="attend_back",
    )
    returned = [partner(sent[k - 1], "dp", k) for k in (1, 2, 3)]

    (ffn_part,) = call(
        functools.partial(down_kernel, split), meta, (act, down_weight),
        [whole(act.shape), block((TILE, D), lambda t, m: (t, 0))],
        [shaped((TOK, D), BF)], [whole((TOK, D))],
        grid=(HF // TILE,), scratch=[pltpu.VMEM((TOK, D), F32)], flops=2 * TOK * D * HF, name="down",
    )
    ffn_there = partner(ffn_part, "mp", 1)
    (block_out,) = simple(block_out_kernel, meta, (hidden, ffn_part, ffn_there), [shaped((TOK, D), BF)], name="block_out")

    if first_radix == outer:
        down_own, down_away = call(
            down_product_kernel, meta,
            tuple([act_pieces[0]] + act_from + [low] + low_from + low_swap),
            [whole((TOK, HF // 4))] * 4 + [whole((TOK, D))] + [whole((TOK, HW))] * 6,
            [shaped((hidden_rows, D), F32), shaped((outer - 1, hidden_rows, D), BF)],
            [block((hidden_rows, TILE), lambda t, m: (0, t)), block((outer - 1, hidden_rows, TILE), lambda t, m: (0, 0, t))],
            grid=(D // TILE,), scratch=[pltpu.VMEM((3, TOK, D), BF), pltpu.VMEM((outer, hidden_rows, TILE), F32)],
            flops=2 * TOK * D * HF, name="down_product",
        )
        down_own = down_own[None]
        down_away = down_away[:, None]
    else:
        lows = [low] + [
            jnp.where(mp_index == 0, jnp.concatenate([a, b], 1), jnp.concatenate([b, a], 1)) for a, b in zip(low_from, low_swap)
        ]
        found = sum(dot_tn(a, b) for a, b in zip(act_pieces[:1] + act_from, lows))
        cut = found.reshape(first_radix, rest, hidden_rows, D)
        digit = outer_index // rest
        down_own = lax.dynamic_index_in_dim(cut, digit, 0, keepdims=False)
        down_away = jnp.stack(
            [lax.dynamic_index_in_dim(cut, digit ^ m, 0, keepdims=False) for m in range(1, first_radix)]
        ).astype(BF)
    down_sum = outer_steps(down_own, down_away, outer, outer_index)

    def second_stage(kept_x, got_x, kept_y, got_y, name):
        _, _, rows, wide = kept_x.shape
        tall = kept_y.shape[-1]
        outs = [shaped((outer, rows, wide), BF)] * 2 + [shaped((outer, rows, tall), BF)] * 2
        away_x, own_x, away_y, own_y = simple(
            second_kernel, meta, (kept_x, got_x, kept_y, got_y), outs,
            scratch=[pltpu.VMEM(kept_x.shape, F32), pltpu.VMEM(kept_y.shape, F32)], name=name + "_second",
        )
        return own_x, partner(away_x, "dp", 2), own_y, partner(away_y, "dp", 1)

    def third_stage(own_x, got_x, own_y, got_y, name):
        rows = own_x.shape[1]
        columns = own_x.shape[2] + own_y.shape[2]
        own, away = simple(
            functools.partial(third_kernel, first_radix), meta, (own_x, got_x, own_y, got_y),
            [shaped((rest, rows, columns), F32), shaped((first_radix - 1, rest, rows, columns), BF)],
            scratch=[pltpu.VMEM((outer, rows, columns), F32)], name=name + "_third",
        )
        return outer_steps(own, away, outer, outer_index)

    up_sum = third_stage(*second_stage(up_kept_x, up_got_x, up_kept_y, up_got_y, "up"), "up")

    qkv_rows = 3 * D // count
    qkv_half = [shaped((outer, 2, qkv_rows, HW // 2), BF)] * 2

    def qkv_product(axis, at):
        return call(
            functools.partial(qkv_product_kernel, axis), meta, (normed, normed_prompt, local),
            [whole((TOK, D)), whole((PMAX, D)), block((1, KEYS, HW // 2), lambda c, m: (c, 0, at))],
            qkv_half, [whole(item.shape) for item in qkv_half],
            grid=(3,), scratch=[pltpu.VMEM((D, KEYS), BF), pltpu.VMEM((3 * D, HW // 2), BF)],
            flops=2 * KEYS * D * 3 * HW // 2, name="qkv_product_" + axis,
        )

    qkv_away_x, qkv_kept_x = qkv_product("x", 0)
    qkv_got_x = partner(qkv_away_x, "dp", 1)
    qkv_away_y, qkv_kept_y = qkv_product("y", 1)
    qkv_got_y = partner(qkv_away_y, "dp", 2)

    (normed_part,) = call(
        grad_normed_kernel, meta, (local, *returned, qkv_weight),
        [block((1, KEYS, HW), lambda c, m: (c, 0, 0))] + [whole((2, PMAX, HW))] * 3 + [block((1, D, HW), lambda c, m: (c, 0, 0))],
        [shaped((TOK, D), BF)], [whole((TOK, D))],
        grid=(3,), scratch=[pltpu.VMEM((PMAX, HW), BF), pltpu.VMEM((TOK, D), F32)],
        flops=2 * KEYS * D * 3 * HW, name="grad_normed",
    )
    normed_there = partner(normed_part, "mp", 1)
    input_grad, tables_first = simple(
        input_grad_kernel, meta, (normed_part, normed_there, tokens, norm_gain, grad_hidden),
        [shaped((TOK, D), BF), shaped((2, D), F32)], name="input_grad",
    )
    qkv_sum = third_stage(*second_stage(qkv_kept_x, qkv_got_x, qkv_kept_y, qkv_got_y, "qkv"), "qkv")

    out_rows = HW // count
    selector = (jnp.arange(SECTIONS) == codebook_section[0]).astype(F32)
    tables = jnp.stack([tables_first, tables_second])
    tables = lax.dynamic_slice_in_dim(tables, mp_index * HW, HW, 2)
    spread = selector[None, None, :, None] * jnp.transpose(tables, (1, 0, 2))[:, :, None, :]
    entries = 2 * SECTIONS * HW // count
    spread = jnp.transpose(spread.reshape(2, count, entries), (1, 0, 2)).reshape(count, 2 * entries // 128, 128).astype(BF)
    spread = jnp.pad(spread, ((0, 0), (0, out_rows - 2 * entries // 128), (0, 0)))
    wide, tall = HW + 128, HW
    away_x, kept_x, away_y, kept_y = simple(
        out_product_kernel, meta, (attended_t, hidden_low, spread),
        [shaped((outer, 2, out_rows, wide), BF)] * 2 + [shaped((outer, 2, out_rows, tall), BF)] * 2,
        scratch=[pltpu.VMEM((outer, 2, 2, out_rows, wide), BF), pltpu.VMEM((outer, 2, 2, out_rows, tall), BF)],
        flops=2 * TOK * HW * D, name="out_product",
    )
    out_sum = third_stage(
        *second_stage(kept_x, partner(away_x, "dp", 1), kept_y, partner(away_y, "dp", 2), "out"), "out"
    )

    flat = master.shape[1]
    received = len(down_sum[1])
    ins = []
    for own, got in (qkv_sum, out_sum, up_sum, down_sum):
        ins += [own, jnp.stack(got)]
    gradient, squares = simple(
        functools.partial(finish_kernel, received), meta, ins,
        [shaped((flat // 128, 128), F32), shaped((8, 128), F32)], name="finish",
    )
    squares = squares + partner(squares, "mp", 1)
    step = 1
    while step < count:
        squares = squares + partner(squares, "dp", step)
        step *= 2
    grad_norm = jnp.sqrt(squares[0, :1])
    step_count = adam_step[0].astype(F32)
    fixes = jnp.stack([1.0 / (1.0 - jnp.power(BETA_ONE, step_count)), 1.0 / (1.0 - jnp.power(BETA_TWO, step_count))]).reshape(1, 2)
    lines = flat // 128
    sizes = [qkv_rows * HW, out_rows * D, up_rows * HF, hidden_rows * D, entries, entries]
    bounds, at = [], 0
    for size in sizes[:-1]:
        at += size // 128 if size % 128 == 0 else 0
        bounds.append(at)
    rates = [D ** (-0.5), OUT_FAN ** (-0.5), D ** (-0.5), FF ** (-0.5), 0.2, 0.2]
    grid = next((g for g in (7, 5, 1) if lines % (8 * g) == 0), 1)
    chunk = block((lines // grid, 128), lambda t, m: (t, 0))
    flats = [item.reshape(lines, 128) for item in (master, first_moment, second_moment, ema_weight)]
    new_first, new_second, new_master, copy, new_ema = call(
        functools.partial(adam_kernel, bounds, rates), meta, (squares, fixes, gradient, *flats),
        [whole((8, 128)), whole((1, 2))] + [chunk] * 5,
        [shaped((lines, 128), F32)] * 3 + [shaped((lines, 128), BF), shaped((lines, 128), F32)],
        [chunk] * 5, grid=(grid,), name="adam",
    )
    return (
        block_out,
        input_grad,
        grad_norm,
        new_first.reshape(1, flat),
        new_second.reshape(1, flat),
        new_master.reshape(1, flat),
        copy.reshape(1, flat),
        new_ema.reshape(1, flat),
    )


def solution(mesh):
    placed = (
        P("dp", None), P("dp", None), P(None, None, "mp"), P("mp", None), P(None, "mp"), P("mp", None), P(), P(),
        P("dp"), P("dp"), P("dp"), P("dp"), P(),
        P("mp", "dp"), P("mp", "dp"), P("mp", "dp"), P("mp", "dp"),
    )
    flat = P("mp", "dp")
    return jax.shard_map(
        body, mesh=mesh, in_specs=placed,
        out_specs=(P("dp", None), P("dp", None), P(), flat, flat, flat, flat, flat),
        check_vma=False,
    )
```

time: 1100 us -> 255 us (0.23)
  waiting for transfers between devices: 793 us -> 73.2 us
  Pallas kernels: 0 us -> 76.8 us
  matrix products: 74.7 us -> 0 us
  other arithmetic: 52.2 us -> 2.62 us
  blocking collectives: 39.6 us -> 0 us
  local copies, waits for them, and re-layouts: 71.7 us -> 35.8 us
  starting transfers between devices: 39.1 us -> 59.2 us
  between operations: 20.3 us -> 6.68 us
    unnamed x7 -> x0, waiting for transfers between devices: 751 us -> none
    pallas_call x0 -> x25, Pallas kernels: none -> 76.8 us  [call(): pl.pallas_call(kernel, grid_spec=pltpu.PrefetchScalarGridSpec(num_scalar_...]
    dot_general x21 -> x0, matrix products: 74.7 us -> none  [the longest x1 11.1 us: body(): pre_act = jnp.dot(second_low, up_weight, preferred_element_type=jnp.float32)]
    ppermute x12 -> x49, waiting for transfers between devices: 7.3 us -> 73.2 us  [partner(): return lax.ppermute(value, axis, [(i, i ^ flip) for i in range(count)])]
    psum x1 -> x0, blocking collectives: 39.6 us -> none  [body(): square_sum = lax.psum(jnp.sum(gradient * gradient), ('dp', 'mp'))]
    psum x3 -> x0, waiting for transfers between devices: 35 us -> none  [the longest x1 21 us: body(): lax.psum(jnp.dot(attended_flat, out_weight, preferred_element_type=jnp.fl...]
    ppermute x12 -> x49, starting transfers between devices: 38.1 us -> 59.2 us  [partner(): return lax.ppermute(value, axis, [(i, i ^ flip) for i in range(count)])]
    reshape x4 -> x0, local copies, waits for them, and re-layouts: 20.6 us -> none  [as_rows(): return matrix.reshape(splits, -1)]
  transfers between devices with their start and end apart: 17 -> 49, of which waited for: 6 -> 18; matrix products, arithmetic and copies ran while one was open for 8% -> 3% of each run, Pallas kernels for 0% -> 21%
where the time goes in v1:
time: 255 us; the launch traced here: 254 us
  Pallas kernels  76.8 us (30%)
  waiting for transfers between devices  73.2 us (29%)
  starting transfers between devices  59.2 us (23%)
  local copies, waits for them, and re-layouts  35.8 us (14%)
  between operations  6.68 us (3%)
  other arithmetic  2.62 us (1%)
    pallas_call x25, Pallas kernels, call(): pl.pallas_call(kernel, grid_spec=pltpu.PrefetchScalarGridSpec(num_scalar_...  76.8 us
    ppermute x49, waiting for transfers between devices, partner(): return lax.ppermute(value, axis, [(i, i ^ flip) for i in range(count)])  73.2 us
    ppermute x49, starting transfers between devices, partner(): return lax.ppermute(value, axis, [(i, i ^ flip) for i in range(count)])  59.2 us
    unnamed x131, local copies, waits for them, and re-layouts  30.2 us
  transfers between devices with their start and end apart: 49, of which 18 were waited for; matrix products, arithmetic and copies ran while one was open for 3% of the time, Pallas kernels for 21%

profile of v1, /device:TPU:0, one launch (start us, length us, event | category | flops | bytes accessed | tf_op | source)
XLA Modules:
  0.0 254.4 jit_solution(2896572534619349653)
XLA Ops:
  6.9 3.0 %collective-permute-start = (bf16[48,1024]{1,0:T(8,128)(2,1)S(1)}, bf16[48,1024]{1,0:T(8,128)(2,1)S(1)}, u32[]{:S(2)}, u32[]{:S(2)}) collective-permute-start(bf16[48,1024]{1,0:T(8,128)(2,1)S(1)} %prompt_norm.1), channel_id=1, source_target_pairs={{0,2},{2,0},{4,6},{6,4},{8,10},{10,8},{12,14},{14,12},{16,18},{18,... | collective-permute-start | bytes 294920 | tf_op jit(solution)/shard_map/ppermute | solution.py:454
  9.9 1.5 collective-permute-start.1
  11.5 1.5 collective-permute-done
  13.0 2.6 %collective-permute-done.1 = bf16[48,1024]{1,0:T(8,128)(2,1)S(1)} collective-permute-done((bf16[48,1024]{1,0:T(8,128)(2,1)S(1)}, bf16[48,1024]{1,0:T(8,128)(2,1)S(1)}, u32[]{:S(2)}, u32[]{:S(2)}) %collective-permute-start.1) | collective-permute-done | bytes 98336 | tf_op jit(solution)/shard_map/ppermute | solution.py:454
  17.1 1.9 copy-done.2
  21.8 2.9 %qkv.3 = (bf16[384,1024]{1,0:T(8,128)(2,1)S(1)}, bf16[3,384,512]{2,1,0:T(8,128)(2,1)S(1)}) custom-call(s32[9]{0:T(128)S(1)} %stack.85.meta, bf16[384,1024]{1,0:T(8,128)(2,1)S(1)} %copy-done.7, f32[2,8,1024]{2,1,0:T(8,128)S(1)} %copy-done.34, f32[2,8,1024]{2,1,0:T(8,128)S(1)} %copy-done.40, bf16[3,1024,512]{2,1,0:T(8,128)(2,1)S(1)} %copy-done.2), custom_call_target="tpu_custom_call" | custom-call | flops 1207959552 | bytes 6029312 | tf_op jit(solution)/shard_map/qkv/pallas_call | solution.py:59
  24.7 5.5 %attend.1 = (bf16[96,1024]{1,0:T(8,128)(2,1)S(1)}, bf16[2,96,512]{2,1,0:T(8,128)(2,1)S(1)}, bf16[512,384]{1,0:T(8,128)(2,1)S(1)}, f32[8,384]{1,0:T(8,128)S(1)}, bf16[384,1024]{1,0:T(8,128)(2,1)S(1)}) custom-call(s32[9]{0:T(128)S(1)} %stack.85.meta, bf16[3,384,512]{2,1,0:T(8,128)(2,1)S(1)} %get-tuple-element.68.projected, ...), custom_call_target="tpu_custom_call" | custom-call | flops 1157627904 | bytes 7155712 | tf_op jit(solution)/shard_map/attend/pallas_call | solution.py:59
  31.6 3.2 %grad_act.1 = f32[384,2048]{1,0:T(8,128)S(1)} custom-call(s32[9]{0:T(128)S(1)} %stack.85.meta, bf16[384,1024]{1,0:T(8,128)(2,1)S(1)} %get-tuple-element.70.low, bf16[2048,1024]{1,0:T(8,128)(2,1)S(1)} %copy-done), custom_call_target="tpu_custom_call" | custom-call | flops 1610612736 | bytes 8126464 | tf_op jit(solution)/shard_map/grad_act/pallas_call | solution.py:59
  34.8 11.2 %ffn.1 = (f32[384,1024]{1,0:T(8,128)S(1)}, bf16[384,1024]{1,0:T(8,128)(2,1)S(1)}, bf16[4,384,512]{2,1,0:T(8,128)(2,1)S(1)}, bf16[384,2048]{1,0:T(8,128)(2,1)S(1)}, bf16[384,1024]{1,0:T(8,128)(2,1)S(1)}) custom-call(s32[9]{0:T(128)S(1)} %stack.85.meta, bf16[384,1024]{1,0:T(8,128)(2,1)S(1)} %copy-done.8, bf16[384,1024]{1,0:T(8,128)(2,1)S(1)} %get-tuple-element.69.here, ...), custom_call_target="tpu_custom_call" | custom-call | flops 3221225472 | bytes 16121856 | tf_op jit(solution)/shard_map/ffn/pallas_call | solution.py:59
  47.7 2.0 collective-permute-start.37
  49.7 3.0 %up_product_x.1 = (bf16[4,2,64,1024]{3,2,1,0:T(8,128)(2,1)S(1)}, bf16[4,2,64,1024]{3,2,1,0:T(8,128)(2,1)S(1)}) custom-call(s32[9]{0:T(128)S(1)} %stack.85.meta, bf16[384,1024]{1,0:T(8,128)(2,1)S(1)} %get-tuple-element.106.normed, bf16[384,2048]{1,0:T(8,128)(2,1)S(1)} %get-tuple-element.107.pre_low), custom_call_target="tpu_custom_call" | custom-call | flops 805306368 | bytes 4456448 | tf_op jit(solution)/shard_map/up_product_x/pallas_call | solution.py:59
  52.7 3.2 %up_product_y.1 = (bf16[4,2,64,1024]{3,2,1,0:T(8,128)(2,1)S(1)}, bf16[4,2,64,1024]{3,2,1,0:T(8,128)(2,1)S(1)}) custom-call(s32[9]{0:T(128)S(1)} %stack.85.meta, bf16[384,1024]{1,0:T(8,128)(2,1)S(1)} %get-tuple-element.106.normed, bf16[384,2048]{1,0:T(8,128)(2,1)S(1)} %get-tuple-element.107.pre_low), custom_call_target="tpu_custom_call" | custom-call | flops 805306368 | bytes 4456448 | tf_op jit(solution)/shard_map/up_product_y/pallas_call | solution.py:59
  59.0 7.9 %collective-permute-done.37.low_c = bf16[384,512]{1,0:T(8,128)(2,1)S(1)} collective-permute-done((bf16[384,512]{1,0:T(8,128)(2,1)S(1)}, bf16[384,512]{1,0:T(8,128)(2,1)S(1)}, u32[]{:S(2)}, u32[]{:S(2)}) %collective-permute-start.37) | collective-permute-done | bytes 393248 | tf_op jit(solution)/shard_map/ppermute | solution.py:454
  67.5 7.9 %attend_back.1 = (bf16[3,480,512]{2,1,0:T(8,128)(2,1)S(1)}, bf16[3,2,96,512]{3,2,1,0:T(8,128)(2,1)S(1)}, f32[384,1024]{1,0:T(8,128)S(1)}, bf16[384,1024]{1,0:T(8,128)(2,1)S(1)}, f32[2,1024]{1,0:T(2,128)S(1)}) custom-call(s32[9]{0:T(128)S(1)} %stack.85.meta, bf16[384,1024]{1,0:T(8,128)(2,1)S(1)} %get-tuple-element.73.here, ...), custom_call_target="tpu_custom_call" | custom-call | flops 2290089984 | bytes 10866688 | tf_op jit(solution)/shard_map/attend_back/pallas_call | solution.py:59
  76.4 1.6 collective-permute-start.7
  82.1 11.2 %collective-permute-done.7.first = bf16[2,96,512]{2,1,0:T(8,128)(2,1)S(1)} collective-permute-done((bf16[2,96,512]{2,1,0:T(8,128)(2,1)S(1)}, bf16[2,96,512]{2,1,0:T(8,128)(2,1)S(1)}, u32[]{:S(2)}, u32[]{:S(2)}) %collective-permute-start.7) | collective-permute-done | bytes 196640 | tf_op jit(solution)/shard_map/ppermute | solution.py:454
  98.0 1.7 collective-permute-start.9
  104.5 2.4 qkv_product_y.1
  106.9 2.4 qkv_product_x.1
  110.8 4.1 %collective-permute-done.8.second = bf16[2,96,512]{2,1,0:T(8,128)(2,1)} collective-permute-done((bf16[2,96,512]{2,1,0:T(8,128)(2,1)}, bf16[2,96,512]{2,1,0:T(8,128)(2,1)}, u32[]{:S(2)}, u32[]{:S(2)}) %collective-permute-start.8) | collective-permute-done | bytes 196640 | tf_op jit(solution)/shard_map/ppermute | solution.py:454
  116.1 2.2 collective-permute-start.28
  118.3 4.8 %grad_normed.1.here = bf16[384,1024]{1,0:T(8,128)(2,1)S(1)} custom-call(s32[9]{0:T(128)S(1)} %stack.85.meta, bf16[3,480,512]{2,1,0:T(8,128)(2,1)S(1)} %copy-done.20, bf16[2,96,512]{2,1,0:T(8,128)(2,1)S(1)} %copy-done.38, bf16[2,96,512]{2,1,0:T(8,128)(2,1)} %collective-permute-done.8.second, bf16[2,96,512]{2,1,0:T(8,128)(2,1)} %collective-permute-done.9.third, ...), custom_call_target="tpu_custom_call" | custom-call | flops 1509949440 | bytes 5996544 | tf_op jit(solution)/shard_map/grad_normed/pallas_call | solution.py:59
  124.5 5.3 %down_product.1 = (f32[128,1024]{1,0:T(8,128)S(1)}, bf16[3,128,1024]{2,1,0:T(8,128)(2,1)S(1)}) custom-call(s32[9]{0:T(128)S(1)} %stack.85.meta, bf16[384,512]{1,0:T(8,128)(2,1)S(1)} %get-tuple-element.131.mine, bf16[384,512]{1,0:T(8,128)(2,1)} %collective-permute-done.32.act_a, bf16[384,512]{1,0:T(8,128)(2,1)} %collective-permute-done.33.act_b, ...), custom_call_target="tpu_custom_call" | custom-call | flops 1610612736 | bytes 6029312 | tf_op jit(solution)/shard_map/down_product/pallas_call | solution.py:59
  130.7 1.5 collective-permute-start.41
  132.1 2.6 %collective-permute-start.42 = (bf16[1,128,1024]{2,1,0:T(8,128)(2,1)}, bf16[1,128,1024]{2,1,0:T(8,128)(2,1)}, u32[]{:S(2)}, u32[]{:S(2)}) collective-permute-start(bf16[1,128,1024]{2,1,0:T(8,128)(2,1)} %get-tuple-element.134), channel_id=1, source_target_pairs={{0,16},{2,18},{4,20},{6,22},{8,24},{10,26},{12,28},{14,30},{16,0},... | collective-permute-start | bytes 786440 | tf_op jit(solution)/shard_map/ppermute | solution.py:454
  136.6 6.1 %collective-permute-done.12.got_y = bf16[4,2,192,256]{3,2,1,0:T(8,128)(2,1)S(1)} collective-permute-done((bf16[4,2,192,256]{3,2,1,0:T(8,128)(2,1)S(1)}, bf16[4,2,192,256]{3,2,1,0:T(8,128)(2,1)S(1)}, u32[]{:S(2)}, u32[]{:S(2)}) %collective-permute-start.12) | collective-permute-done | bytes 786464 | tf_op jit(solution)/shard_map/ppermute | solution.py:454
  142.7 3.7 %collective-permute-start.43 = (bf16[1,128,1024]{2,1,0:T(8,128)(2,1)}, bf16[1,128,1024]{2,1,0:T(8,128)(2,1)}, u32[]{:S(2)}, u32[]{:S(2)}) collective-permute-start(bf16[1,128,1024]{2,1,0:T(8,128)(2,1)} %get-tuple-element.133), channel_id=1, source_target_pairs={{0,24},{2,26},{4,28},{6,30},{8,16},{10,18},{12,20},{14,22},{16,8},... | collective-permute-start | bytes 786440 | tf_op jit(solution)/shard_map/ppermute | solution.py:454
  146.4 2.6 %collective-permute-start.30 = (bf16[1,64,2048]{2,1,0:T(8,128)(2,1)}, bf16[1,64,2048]{2,1,0:T(8,128)(2,1)}, u32[]{:S(2)}, u32[]{:S(2)}) collective-permute-start(bf16[1,64,2048]{2,1,0:T(8,128)(2,1)} %get-tuple-element.137), channel_id=1, source_target_pairs={{0,16},{2,18},{4,20},{6,22},{8,24},{10,26},{12,28},{14,30},{16,0},... | collective-permute-start | bytes 786440 | tf_op jit(solution)/shard_map/ppermute | solution.py:454
  149.0 5.2 %down.4.here = bf16[384,1024]{1,0:T(8,128)(2,1)S(1)} custom-call(s32[9]{0:T(128)S(1)} %stack.85.meta, bf16[4,384,512]{2,1,0:T(8,128)(2,1)S(1)} %copy-done.5, bf16[2048,1024]{1,0:T(8,128)(2,1)S(1)} %copy-done.1), custom_call_target="tpu_custom_call" | custom-call | flops 1610612736 | bytes 6553600 | tf_op jit(solution)/shard_map/down/pallas_call | solution.py:59
  156.2 2.8 %input_grad.1 = (bf16[384,1024]{1,0:T(8,128)(2,1)}, f32[2,1024]{1,0:T(2,128)S(1)}) custom-call(s32[9]{0:T(128)S(1)} %stack.85.meta, bf16[384,1024]{1,0:T(8,128)(2,1)S(1)} %grad_normed.1.here, bf16[384,1024]{1,0:T(8,128)(2,1)S(1)} %collective-permute-done.10.there, bf16[384,1024]{1,0:T(8,128)(2,1)S(1)} %copy-done.9, f32[2,8,1024]{2,1,0:T(8,128)S(1)} %copy-done.36, ...), custom_call_target="tpu_custom_call" | custom-call | bytes 4792320 | tf_op jit(solution)/shard_map/input_grad/pallas_call | solution.py:59
  159.1 1.8 collective-permute-start.31
  166.7 9.2 %collective-permute-done.30 = bf16[1,64,2048]{2,1,0:T(8,128)(2,1)} collective-permute-done((bf16[1,64,2048]{2,1,0:T(8,128)(2,1)}, bf16[1,64,2048]{2,1,0:T(8,128)(2,1)}, u32[]{:S(2)}, u32[]{:S(2)}) %collective-permute-start.30) | collective-permute-done | bytes 262176 | tf_op jit(solution)/shard_map/ppermute | solution.py:454
  180.3 3.4 %collective-permute-done.19.got_y = bf16[4,2,32,512]{3,2,1,0:T(8,128)(2,1)S(1)} collective-permute-done((bf16[4,2,32,512]{3,2,1,0:T(8,128)(2,1)S(1)}, bf16[4,2,32,512]{3,2,1,0:T(8,128)(2,1)S(1)}, u32[]{:S(2)}, u32[]{:S(2)}) %collective-permute-start.19) | collective-permute-done | bytes 262176 | tf_op jit(solution)/shard_map/ppermute | solution.py:454
  185.6 1.8 collective-permute-start.21
  187.4 4.8 %collective-permute-start.15 = (bf16[1,192,512]{2,1,0:T(8,128)(2,1)S(1)}, bf16[1,192,512]{2,1,0:T(8,128)(2,1)S(1)}, u32[]{:S(2)}, u32[]{:S(2)}) collective-permute-start(bf16[1,192,512]{2,1,0:T(8,128)(2,1)S(1)} %get-tuple-element.138), channel_id=1, source_target_pairs={{0,8},{2,10},{4,12},{6,14},{8,0},{10,2},{12,4},{14,6},{16,24},{18,... | collective-permute-start | bytes 589832 | tf_op jit(solution)/shard_map/ppermute | solution.py:454
  192.7 2.0 collective-permute-start.17
  195.4 1.8 collective-permute-start.22
  197.2 3.7 %collective-permute-done.15 = bf16[1,192,512]{2,1,0:T(8,128)(2,1)S(1)} collective-permute-done((bf16[1,192,512]{2,1,0:T(8,128)(2,1)S(1)}, bf16[1,192,512]{2,1,0:T(8,128)(2,1)S(1)}, u32[]{:S(2)}, u32[]{:S(2)}) %collective-permute-start.15) | collective-permute-done | bytes 196640 | tf_op jit(solution)/shard_map/ppermute | solution.py:454
  200.9 7.5 %collective-permute-done.16 = bf16[1,192,512]{2,1,0:T(8,128)(2,1)S(1)} collective-permute-done((bf16[1,192,512]{2,1,0:T(8,128)(2,1)S(1)}, bf16[1,192,512]{2,1,0:T(8,128)(2,1)S(1)}, u32[]{:S(2)}, u32[]{:S(2)}) %collective-permute-start.16) | collective-permute-done | bytes 196640 | tf_op jit(solution)/shard_map/ppermute | solution.py:454
  208.4 3.9 %collective-permute-start.24 = (bf16[1,32,1152]{2,1,0:T(8,128)(2,1)S(1)}, bf16[1,32,1152]{2,1,0:T(8,128)(2,1)S(1)}, u32[]{:S(2)}, u32[]{:S(2)}) collective-permute-start(bf16[1,32,1152]{2,1,0:T(8,128)(2,1)S(1)} %get-tuple-element.145), channel_id=1, source_target_pairs={{0,24},{2,26},{4,28},{6,30},{8,16},{10,18},{12,20},{14,22},{16,8},... | collective-permute-start | bytes 221192 | tf_op jit(solution)/shard_map/ppermute | solution.py:454
  212.4 3.3 %collective-permute-done.23 = bf16[1,32,1152]{2,1,0:T(8,128)(2,1)S(1)} collective-permute-done((bf16[1,32,1152]{2,1,0:T(8,128)(2,1)S(1)}, bf16[1,32,1152]{2,1,0:T(8,128)(2,1)S(1)}, u32[]{:S(2)}, u32[]{:S(2)}) %collective-permute-start.23) | collective-permute-done | bytes 73760 | tf_op jit(solution)/shard_map/ppermute | solution.py:454
  215.9 1.5 finish.1
  219.1 3.1 %collective-permute-done.45 = f32[8,128]{1,0:T(8,128)S(1)} collective-permute-done((f32[8,128]{1,0:T(8,128)S(1)}, f32[8,128]{1,0:T(8,128)S(1)}, u32[]{:S(2)}, u32[]{:S(2)}) %collective-permute-start.45) | collective-permute-done | bytes 4128 | tf_op jit(solution)/shard_map/ppermute | solution.py:454
  222.9 2.9 %collective-permute-done.46 = f32[8,128]{1,0:T(8,128)S(1)} collective-permute-done((f32[8,128]{1,0:T(8,128)S(1)}, f32[8,128]{1,0:T(8,128)S(1)}, u32[]{:S(2)}, u32[]{:S(2)}) %collective-permute-start.46) | collective-permute-done | bytes 4128 | tf_op jit(solution)/shard_map/ppermute | solution.py:454
  225.8 1.5 collective-permute-start.47
  230.7 1.7 block_out.1
  234.4 5.2 %adam.1 = (f32[3080,128]{1,0:T(8,128)}, f32[3080,128]{1,0:T(8,128)}, f32[3080,128]{1,0:T(8,128)}, bf16[3080,128]{1,0:T(8,128)(2,1)S(1)}, f32[3080,128]{1,0:T(8,128)}) custom-call(s32[9]{0:T(128)S(1)} %stack.85.meta, f32[8,128]{1,0:T(8,128)S(1)} %add.32.square_sum, f32[1,2]{1,0:T(1,128)S(1)} %maximum_bitcast_fusion.fixes, ...), custom_call_target="tpu_custom_call" | custom-call | bytes 14985224 | tf_op jit(solution)/shard_map/adam/pallas_call | solution.py:59
  239.6 12.9 %copy.27 = bf16[1,1,3080,128]{3,1,2,0:T(2,128)(2,1)} copy(bf16[1,1,3080,128]{3,2,1,0:T(8,128)(2,1)S(1)} %bitcast.85) | data formatting | bytes 1576960
  (232 shorter events, 58.2 us)
Async XLA Ops:
  6.9 6.1 %collective-permute-start = (bf16[48,1024]{1,0:T(8,128)(2,1)S(1)}, bf16[48,1024]{1,0:T(8,128)(2,1)S(1)}, u32[]{:S(2)}, u32[]{:S(2)}) collective-permute-start(bf16[48,1024]{1,0:T(8,128)(2,1)S(1)} %prompt_norm.1), channel_id=1, source_target_pairs={{0,2},{2,0},{4,6},{6,4},{8,10},{10,8},{12,14},{14,12},{16,18},{18,... | collective-permute-start | bytes 294920 | tf_op jit(solution)/shard_map/ppermute | solution.py:454
  9.9 5.7 %collective-permute-start.1 = (bf16[48,1024]{1,0:T(8,128)(2,1)S(1)}, bf16[48,1024]{1,0:T(8,128)(2,1)S(1)}, u32[]{:S(2)}, u32[]{:S(2)}) collective-permute-start(bf16[48,1024]{1,0:T(8,128)(2,1)S(1)} %prompt_norm.1), channel_id=1, source_target_pairs={{0,4},{2,6},{4,0},{6,2},{8,12},{10,14},{12,8},{14,10},{16,20},{18,... | collective-permute-start | bytes 294920 | tf_op jit(solution)/shard_map/ppermute | solution.py:454
  11.4 5.5 %collective-permute-start.2 = (bf16[48,1024]{1,0:T(8,128)(2,1)S(1)}, bf16[48,1024]{1,0:T(8,128)(2,1)S(1)}, u32[]{:S(2)}, u32[]{:S(2)}) collective-permute-start(bf16[48,1024]{1,0:T(8,128)(2,1)S(1)} %prompt_norm.1), channel_id=1, source_target_pairs={{0,6},{2,4},{4,2},{6,0},{8,14},{10,12},{12,10},{14,8},{16,22},{18,... | collective-permute-start | bytes 294920 | tf_op jit(solution)/shard_map/ppermute | solution.py:454
  17.0 7.7 %collective-permute-start.3 = (bf16[48,1024]{1,0:T(8,128)(2,1)S(1)}, bf16[48,1024]{1,0:T(8,128)(2,1)S(1)}, u32[]{:S(2)}, u32[]{:S(2)}) collective-permute-start(bf16[48,1024]{1,0:T(8,128)(2,1)S(1)} %select_select_fusion.here), channel_id=1, source_target_pairs={{0,1},{1,0},{2,3},{3,2},{4,5},{5,4},{6,7},{7,6},{8,9},{9,8},{10,11... | collective-permute-start | bytes 294920 | tf_op jit(solution)/shard_map/ppermute | solution.py:454
  30.3 4.5 %collective-permute-start.4 = (bf16[384,1024]{1,0:T(8,128)(2,1)S(1)}, bf16[384,1024]{1,0:T(8,128)(2,1)S(1)}, u32[]{:S(2)}, u32[]{:S(2)}) collective-permute-start(bf16[384,1024]{1,0:T(8,128)(2,1)S(1)} %get-tuple-element.69.here), channel_id=1, source_target_pairs={{0,1},{1,0},{2,3},{3,2},{4,5},{5,4},{6,7},{7,6},{8,9},{9,8},{10,11... | collective-permute-start | bytes 2359304 | tf_op jit(solution)/shard_map/ppermute | solution.py:454
  46.0 20.9 %collective-permute-start.6 = (bf16[384,1024]{1,0:T(8,128)(2,1)S(1)}, bf16[384,1024]{1,0:T(8,128)(2,1)S(1)}, u32[]{:S(2)}, u32[]{:S(2)}) collective-permute-start(bf16[384,1024]{1,0:T(8,128)(2,1)S(1)} %get-tuple-element.73.here), channel_id=1, source_target_pairs={{0,1},{1,0},{2,3},{3,2},{4,5},{5,4},{6,7},{7,6},{8,9},{9,8},{10,11... | collective-permute-start | bytes 2359304 | tf_op jit(solution)/shard_map/ppermute | solution.py:454
  46.1 12.0 %collective-permute-start.35 = (bf16[384,512]{1,0:T(8,128)(2,1)S(1)}, bf16[384,512]{1,0:T(8,128)(2,1)S(1)}, u32[]{:S(2)}, u32[]{:S(2)}) collective-permute-start(bf16[384,512]{1,0:T(8,128)(2,1)S(1)} %get-tuple-element.118), channel_id=1, source_target_pairs={{0,2},{2,0},{4,6},{6,4},{8,10},{10,8},{12,14},{14,12},{16,18},{18,... | collective-permute-start | bytes 1179656 | tf_op jit(solution)/shard_map/ppermute | solution.py:454
  46.8 12.2 %collective-permute-start.36 = (bf16[384,512]{1,0:T(8,128)(2,1)S(1)}, bf16[384,512]{1,0:T(8,128)(2,1)S(1)}, u32[]{:S(2)}, u32[]{:S(2)}) collective-permute-start(bf16[384,512]{1,0:T(8,128)(2,1)S(1)} %get-tuple-element.118), channel_id=1, source_target_pairs={{0,4},{2,6},{4,0},{6,2},{8,12},{10,14},{12,8},{14,10},{16,20},{18,... | collective-permute-start | bytes 1179656 | tf_op jit(solution)/shard_map/ppermute | solution.py:454
  47.7 19.2 %collective-permute-start.37 = (bf16[384,512]{1,0:T(8,128)(2,1)S(1)}, bf16[384,512]{1,0:T(8,128)(2,1)S(1)}, u32[]{:S(2)}, u32[]{:S(2)}) collective-permute-start(bf16[384,512]{1,0:T(8,128)(2,1)S(1)} %get-tuple-element.118), channel_id=1, source_target_pairs={{0,6},{2,4},{4,2},{6,0},{8,14},{10,12},{12,10},{14,8},{16,22},{18,... | collective-permute-start | bytes 1179656 | tf_op jit(solution)/shard_map/ppermute | solution.py:454
  56.0 38.9 %collective-permute-start.25 = (bf16[4,2,64,1024]{3,2,1,0:T(8,128)(2,1)S(1)}, bf16[4,2,64,1024]{3,2,1,0:T(8,128)(2,1)S(1)}, u32[]{:S(2)}, u32[]{:S(2)}) collective-permute-start(bf16[4,2,64,1024]{3,2,1,0:T(8,128)(2,1)S(1)} %get-tuple-element.109), channel_id=1, source_target_pairs={{0,2},{2,0},{4,6},{6,4},{8,10},{10,8},{12,14},{14,12},{16,18},{18,... | collective-permute-start | bytes 3145736 | tf_op jit(solution)/shard_map/ppermute | solution.py:454
  58.1 38.9 %collective-permute-start.26 = (bf16[4,2,64,1024]{3,2,1,0:T(8,128)(2,1)S(1)}, bf16[4,2,64,1024]{3,2,1,0:T(8,128)(2,1)S(1)}, u32[]{:S(2)}, u32[]{:S(2)}) collective-permute-start(bf16[4,2,64,1024]{3,2,1,0:T(8,128)(2,1)S(1)} %get-tuple-element.111), channel_id=1, source_target_pairs={{0,4},{2,6},{4,0},{6,2},{8,12},{10,14},{12,8},{14,10},{16,20},{18,... | collective-permute-start | bytes 3145736 | tf_op jit(solution)/shard_map/ppermute | solution.py:454
  59.0 17.3 %collective-permute-start.38 = (bf16[384,512]{1,0:T(8,128)(2,1)S(1)}, bf16[384,512]{1,0:T(8,128)(2,1)S(1)}, u32[]{:S(2)}, u32[]{:S(2)}) collective-permute-start(bf16[384,512]{1,0:T(8,128)(2,1)S(1)} %collective-permute-done.35.low_a), channel_id=1, source_target_pairs={{0,1},{1,0},{2,3},{3,2},{4,5},{5,4},{6,7},{7,6},{8,9},{9,8},{10,11... | collective-permute-start | bytes 1179656 | tf_op jit(solution)/shard_map/ppermute | solution.py:454
  66.9 12.1 %collective-permute-start.39 = (bf16[384,512]{1,0:T(8,128)(2,1)S(1)}, bf16[384,512]{1,0:T(8,128)(2,1)S(1)}, u32[]{:S(2)}, u32[]{:S(2)}) collective-permute-start(bf16[384,512]{1,0:T(8,128)(2,1)S(1)} %collective-permute-done.36.low_b), channel_id=1, source_target_pairs={{0,1},{1,0},{2,3},{3,2},{4,5},{5,4},{6,7},{7,6},{8,9},{9,8},{10,11... | collective-permute-start | bytes 1179656 | tf_op jit(solution)/shard_map/ppermute | solution.py:454
  66.9 13.4 %collective-permute-start.40 = (bf16[384,512]{1,0:T(8,128)(2,1)S(1)}, bf16[384,512]{1,0:T(8,128)(2,1)S(1)}, u32[]{:S(2)}, u32[]{:S(2)}) collective-permute-start(bf16[384,512]{1,0:T(8,128)(2,1)S(1)} %collective-permute-done.37.low_c), channel_id=1, source_target_pairs={{0,1},{1,0},{2,3},{3,2},{4,5},{5,4},{6,7},{7,6},{8,9},{9,8},{10,11... | collective-permute-start | bytes 1179656 | tf_op jit(solution)/shard_map/ppermute | solution.py:454
  76.4 16.9 %collective-permute-start.7 = (bf16[2,96,512]{2,1,0:T(8,128)(2,1)S(1)}, bf16[2,96,512]{2,1,0:T(8,128)(2,1)S(1)}, u32[]{:S(2)}, u32[]{:S(2)}) collective-permute-start(bf16[2,96,512]{2,1,0:T(8,128)(2,1)S(1)} %get-tuple-element.143), channel_id=1, source_target_pairs={{0,2},{2,0},{4,6},{6,4},{8,10},{10,8},{12,14},{14,12},{16,18},{18,... | collective-permute-start | bytes 589832 | tf_op jit(solution)/shard_map/ppermute | solution.py:454
  79.8 43.3 %collective-permute-start.32 = (bf16[384,512]{1,0:T(8,128)(2,1)}, bf16[384,512]{1,0:T(8,128)(2,1)}, u32[]{:S(2)}, u32[]{:S(2)}) collective-permute-start(bf16[384,512]{1,0:T(8,128)(2,1)} %get-tuple-element.130), channel_id=1, source_target_pairs={{0,2},{2,0},{4,6},{6,4},{8,10},{10,8},{12,14},{14,12},{16,18},{18,... | collective-permute-start | bytes 1179656 | tf_op jit(solution)/shard_map/ppermute | solution.py:454
  81.1 43.1 %collective-permute-start.33 = (bf16[384,512]{1,0:T(8,128)(2,1)}, bf16[384,512]{1,0:T(8,128)(2,1)}, u32[]{:S(2)}, u32[]{:S(2)}) collective-permute-start(bf16[384,512]{1,0:T(8,128)(2,1)} %get-tuple-element.129), channel_id=1, source_target_pairs={{0,4},{2,6},{4,0},{6,2},{8,12},{10,14},{12,8},{14,10},{16,20},{18,... | collective-permute-start | bytes 1179656 | tf_op jit(solution)/shard_map/ppermute | solution.py:454
  93.9 30.5 %collective-permute-start.34 = (bf16[384,512]{1,0:T(8,128)(2,1)}, bf16[384,512]{1,0:T(8,128)(2,1)}, u32[]{:S(2)}, u32[]{:S(2)}) collective-permute-start(bf16[384,512]{1,0:T(8,128)(2,1)} %get-tuple-element.128), channel_id=1, source_target_pairs={{0,6},{2,4},{4,2},{6,0},{8,14},{10,12},{12,10},{14,8},{16,22},{18,... | collective-permute-start | bytes 1179656 | tf_op jit(solution)/shard_map/ppermute | solution.py:454
  95.9 19.0 %collective-permute-start.8 = (bf16[2,96,512]{2,1,0:T(8,128)(2,1)}, bf16[2,96,512]{2,1,0:T(8,128)(2,1)}, u32[]{:S(2)}, u32[]{:S(2)}) collective-permute-start(bf16[2,96,512]{2,1,0:T(8,128)(2,1)} %get-tuple-element.142), channel_id=1, source_target_pairs={{0,4},{2,6},{4,0},{6,2},{8,12},{10,14},{12,8},{14,10},{16,20},{18,... | collective-permute-start | bytes 589832 | tf_op jit(solution)/shard_map/ppermute | solution.py:454
  98.0 18.1 %collective-permute-start.9 = (bf16[2,96,512]{2,1,0:T(8,128)(2,1)}, bf16[2,96,512]{2,1,0:T(8,128)(2,1)}, u32[]{:S(2)}, u32[]{:S(2)}) collective-permute-start(bf16[2,96,512]{2,1,0:T(8,128)(2,1)} %get-tuple-element.141), channel_id=1, source_target_pairs={{0,6},{2,4},{4,2},{6,0},{8,14},{10,12},{12,10},{14,8},{16,22},{18,... | collective-permute-start | bytes 589832 | tf_op jit(solution)/shard_map/ppermute | solution.py:454
  114.9 15.8 %collective-permute-start.27 = (bf16[4,64,1024]{2,1,0:T(8,128)(2,1)S(1)}, bf16[4,64,1024]{2,1,0:T(8,128)(2,1)S(1)}, u32[]{:S(2)}, u32[]{:S(2)}) collective-permute-start(bf16[4,64,1024]{2,1,0:T(8,128)(2,1)S(1)} %get-tuple-element.113), channel_id=1, source_target_pairs={{0,4},{2,6},{4,0},{6,2},{8,12},{10,14},{12,8},{14,10},{16,20},{18,... | collective-permute-start | bytes 1572872 | tf_op jit(solution)/shard_map/ppermute | solution.py:454
  116.1 16.0 %collective-permute-start.28 = (bf16[4,64,1024]{2,1,0:T(8,128)(2,1)S(1)}, bf16[4,64,1024]{2,1,0:T(8,128)(2,1)S(1)}, u32[]{:S(2)}, u32[]{:S(2)}) collective-permute-start(bf16[4,64,1024]{2,1,0:T(8,128)(2,1)S(1)} %get-tuple-element.115), channel_id=1, source_target_pairs={{0,2},{2,0},{4,6},{6,4},{8,10},{10,8},{12,14},{14,12},{16,18},{18,... | collective-permute-start | bytes 1572872 | tf_op jit(solution)/shard_map/ppermute | solution.py:454
  123.1 19.5 %collective-permute-start.12 = (bf16[4,2,192,256]{3,2,1,0:T(8,128)(2,1)S(1)}, bf16[4,2,192,256]{3,2,1,0:T(8,128)(2,1)S(1)}, u32[]{:S(2)}, u32[]{:S(2)}) collective-permute-start(bf16[4,2,192,256]{3,2,1,0:T(8,128)(2,1)S(1)} %get-tuple-element.85), channel_id=1, source_target_pairs={{0,4},{2,6},{4,0},{6,2},{8,12},{10,14},{12,8},{14,10},{16,20},{18,... | collective-permute-start | bytes 2359304 | tf_op jit(solution)/shard_map/ppermute | solution.py:454
  124.2 22.2 %collective-permute-start.11 = (bf16[4,2,192,256]{3,2,1,0:T(8,128)(2,1)S(1)}, bf16[4,2,192,256]{3,2,1,0:T(8,128)(2,1)S(1)}, u32[]{:S(2)}, u32[]{:S(2)}) collective-permute-start(bf16[4,2,192,256]{3,2,1,0:T(8,128)(2,1)S(1)} %get-tuple-element.83), channel_id=1, source_target_pairs={{0,2},{2,0},{4,6},{6,4},{8,10},{10,8},{12,14},{14,12},{16,18},{18,... | collective-permute-start | bytes 2359304 | tf_op jit(solution)/shard_map/ppermute | solution.py:454
  124.4 22.0 %collective-permute-start.10 = (bf16[384,1024]{1,0:T(8,128)(2,1)S(1)}, bf16[384,1024]{1,0:T(8,128)(2,1)S(1)}, u32[]{:S(2)}, u32[]{:S(2)}) collective-permute-start(bf16[384,1024]{1,0:T(8,128)(2,1)S(1)} %grad_normed.1.here), channel_id=1, source_target_pairs={{0,1},{1,0},{2,3},{3,2},{4,5},{5,4},{6,7},{7,6},{8,9},{9,8},{10,11... | collective-permute-start | bytes 2359304 | tf_op jit(solution)/shard_map/ppermute | solution.py:454
  130.7 28.4 %collective-permute-start.41 = (bf16[1,128,1024]{2,1,0:T(8,128)(2,1)S(1)}, bf16[1,128,1024]{2,1,0:T(8,128)(2,1)S(1)}, u32[]{:S(2)}, u32[]{:S(2)}) collective-permute-start(bf16[1,128,1024]{2,1,0:T(8,128)(2,1)S(1)} %get-tuple-element.132), channel_id=1, source_target_pairs={{0,8},{2,10},{4,12},{6,14},{8,0},{10,2},{12,4},{14,6},{16,24},{18,... | collective-permute-start | bytes 786440 | tf_op jit(solution)/shard_map/ppermute | solution.py:454
  132.1 28.8 %collective-permute-start.42 = (bf16[1,128,1024]{2,1,0:T(8,128)(2,1)}, bf16[1,128,1024]{2,1,0:T(8,128)(2,1)}, u32[]{:S(2)}, u32[]{:S(2)}) collective-permute-start(bf16[1,128,1024]{2,1,0:T(8,128)(2,1)} %get-tuple-element.134), channel_id=1, source_target_pairs={{0,16},{2,18},{4,20},{6,22},{8,24},{10,26},{12,28},{14,30},{16,0},... | collective-permute-start | bytes 786440 | tf_op jit(solution)/shard_map/ppermute | solution.py:454
  142.7 19.4 %collective-permute-start.43 = (bf16[1,128,1024]{2,1,0:T(8,128)(2,1)}, bf16[1,128,1024]{2,1,0:T(8,128)(2,1)}, u32[]{:S(2)}, u32[]{:S(2)}) collective-permute-start(bf16[1,128,1024]{2,1,0:T(8,128)(2,1)} %get-tuple-element.133), channel_id=1, source_target_pairs={{0,24},{2,26},{4,28},{6,30},{8,16},{10,18},{12,20},{14,22},{16,8},... | collective-permute-start | bytes 786440 | tf_op jit(solution)/shard_map/ppermute | solution.py:454
  146.4 19.6 %collective-permute-start.29 = (bf16[1,64,2048]{2,1,0:T(8,128)(2,1)}, bf16[1,64,2048]{2,1,0:T(8,128)(2,1)}, u32[]{:S(2)}, u32[]{:S(2)}) collective-permute-start(bf16[1,64,2048]{2,1,0:T(8,128)(2,1)} %get-tuple-element.135), channel_id=1, source_target_pairs={{0,8},{2,10},{4,12},{6,14},{8,0},{10,2},{12,4},{14,6},{16,24},{18,... | collective-permute-start | bytes 786440 | tf_op jit(solution)/shard_map/ppermute | solution.py:454
  146.4 29.4 %collective-permute-start.30 = (bf16[1,64,2048]{2,1,0:T(8,128)(2,1)}, bf16[1,64,2048]{2,1,0:T(8,128)(2,1)}, u32[]{:S(2)}, u32[]{:S(2)}) collective-permute-start(bf16[1,64,2048]{2,1,0:T(8,128)(2,1)} %get-tuple-element.137), channel_id=1, source_target_pairs={{0,16},{2,18},{4,20},{6,22},{8,24},{10,26},{12,28},{14,30},{16,0},... | collective-permute-start | bytes 786440 | tf_op jit(solution)/shard_map/ppermute | solution.py:454
  159.1 19.0 %collective-permute-start.31 = (bf16[1,64,2048]{2,1,0:T(8,128)(2,1)}, bf16[1,64,2048]{2,1,0:T(8,128)(2,1)}, u32[]{:S(2)}, u32[]{:S(2)}) collective-permute-start(bf16[1,64,2048]{2,1,0:T(8,128)(2,1)} %get-tuple-element.136), channel_id=1, source_target_pairs={{0,24},{2,26},{4,28},{6,30},{8,16},{10,18},{12,20},{14,22},{16,8},... | collective-permute-start | bytes 786440 | tf_op jit(solution)/shard_map/ppermute | solution.py:454
  161.0 18.4 %collective-permute-start.13 = (bf16[4,192,256]{2,1,0:T(8,128)(2,1)}, bf16[4,192,256]{2,1,0:T(8,128)(2,1)S(1)}, u32[]{:S(2)}, u32[]{:S(2)}) collective-permute-start(bf16[4,192,256]{2,1,0:T(8,128)(2,1)} %copy-done.56), channel_id=1, source_target_pairs={{0,4},{2,6},{4,0},{6,2},{8,12},{10,14},{12,8},{14,10},{16,20},{18,... | collective-permute-start | bytes 1179656 | tf_op jit(solution)/shard_map/ppermute | solution.py:454
  162.1 17.3 %collective-permute-start.14 = (bf16[4,192,256]{2,1,0:T(8,128)(2,1)S(1)}, bf16[4,192,256]{2,1,0:T(8,128)(2,1)S(1)}, u32[]{:S(2)}, u32[]{:S(2)}) collective-permute-start(bf16[4,192,256]{2,1,0:T(8,128)(2,1)S(1)} %get-tuple-element.89), channel_id=1, source_target_pairs={{0,2},{2,0},{4,6},{6,4},{8,10},{10,8},{12,14},{14,12},{16,18},{18,... | collective-permute-start | bytes 1179656 | tf_op jit(solution)/shard_map/ppermute | solution.py:454
  166.0 17.7 %collective-permute-start.18 = (bf16[4,2,32,640]{3,2,1,0:T(8,128)(2,1)S(1)}, bf16[4,2,32,640]{3,2,1,0:T(8,128)(2,1)S(1)}, u32[]{:S(2)}, u32[]{:S(2)}) collective-permute-start(bf16[4,2,32,640]{3,2,1,0:T(8,128)(2,1)S(1)} %get-tuple-element.97), channel_id=1, source_target_pairs={{0,2},{2,0},{4,6},{6,4},{8,10},{10,8},{12,14},{14,12},{16,18},{18,... | collective-permute-start | bytes 983048 | tf_op jit(solution)/shard_map/ppermute | solution.py:454
  175.8 7.8 %collective-permute-start.19 = (bf16[4,2,32,512]{3,2,1,0:T(8,128)(2,1)S(1)}, bf16[4,2,32,512]{3,2,1,0:T(8,128)(2,1)S(1)}, u32[]{:S(2)}, u32[]{:S(2)}) collective-permute-start(bf16[4,2,32,512]{3,2,1,0:T(8,128)(2,1)S(1)} %get-tuple-element.99), channel_id=1, source_target_pairs={{0,4},{2,6},{4,0},{6,2},{8,12},{10,14},{12,8},{14,10},{16,20},{18,... | collective-permute-start | bytes 786440 | tf_op jit(solution)/shard_map/ppermute | solution.py:454
  178.1 52.6 %collective-permute-start.5 = (bf16[384,1024]{1,0:T(8,128)(2,1)S(1)}, bf16[384,1024]{1,0:T(8,128)(2,1)S(1)}, u32[]{:S(2)}, u32[]{:S(2)}) collective-permute-start(bf16[384,1024]{1,0:T(8,128)(2,1)S(1)} %down.4.here), channel_id=1, source_target_pairs={{0,1},{1,0},{2,3},{3,2},{4,5},{5,4},{6,7},{7,6},{8,9},{9,8},{10,11... | collective-permute-start | bytes 2359304 | tf_op jit(solution)/shard_map/ppermute | solution.py:454
  184.4 10.3 %collective-permute-start.20 = (bf16[4,32,640]{2,1,0:T(8,128)(2,1)S(1)}, bf16[4,32,640]{2,1,0:T(8,128)(2,1)S(1)}, u32[]{:S(2)}, u32[]{:S(2)}) collective-permute-start(bf16[4,32,640]{2,1,0:T(8,128)(2,1)S(1)} %get-tuple-element.101), channel_id=1, source_target_pairs={{0,4},{2,6},{4,0},{6,2},{8,12},{10,14},{12,8},{14,10},{16,20},{18,... | collective-permute-start | bytes 491528 | tf_op jit(solution)/shard_map/ppermute | solution.py:454
  185.6 7.1 %collective-permute-start.21 = (bf16[4,32,512]{2,1,0:T(8,128)(2,1)S(1)}, bf16[4,32,512]{2,1,0:T(8,128)(2,1)S(1)}, u32[]{:S(2)}, u32[]{:S(2)}) collective-permute-start(bf16[4,32,512]{2,1,0:T(8,128)(2,1)S(1)} %get-tuple-element.103), channel_id=1, source_target_pairs={{0,2},{2,0},{4,6},{6,4},{8,10},{10,8},{12,14},{14,12},{16,18},{18,... | collective-permute-start | bytes 393224 | tf_op jit(solution)/shard_map/ppermute | solution.py:454
  187.4 13.5 %collective-permute-start.15 = (bf16[1,192,512]{2,1,0:T(8,128)(2,1)S(1)}, bf16[1,192,512]{2,1,0:T(8,128)(2,1)S(1)}, u32[]{:S(2)}, u32[]{:S(2)}) collective-permute-start(bf16[1,192,512]{2,1,0:T(8,128)(2,1)S(1)} %get-tuple-element.138), channel_id=1, source_target_pairs={{0,8},{2,10},{4,12},{6,14},{8,0},{10,2},{12,4},{14,6},{16,24},{18,... | collective-permute-start | bytes 589832 | tf_op jit(solution)/shard_map/ppermute | solution.py:454
  192.2 16.2 %collective-permute-start.16 = (bf16[1,192,512]{2,1,0:T(8,128)(2,1)S(1)}, bf16[1,192,512]{2,1,0:T(8,128)(2,1)S(1)}, u32[]{:S(2)}, u32[]{:S(2)}) collective-permute-start(bf16[1,192,512]{2,1,0:T(8,128)(2,1)S(1)} %get-tuple-element.140), channel_id=1, source_target_pairs={{0,16},{2,18},{4,20},{6,22},{8,24},{10,26},{12,28},{14,30},{16,0},... | collective-permute-start | bytes 589832 | tf_op jit(solution)/shard_map/ppermute | solution.py:454
  192.7 19.7 %collective-permute-start.17 = (bf16[1,192,512]{2,1,0:T(8,128)(2,1)S(1)}, bf16[1,192,512]{2,1,0:T(8,128)(2,1)S(1)}, u32[]{:S(2)}, u32[]{:S(2)}) collective-permute-start(bf16[1,192,512]{2,1,0:T(8,128)(2,1)S(1)} %get-tuple-element.139), channel_id=1, source_target_pairs={{0,24},{2,26},{4,28},{6,30},{8,16},{10,18},{12,20},{14,22},{16,8},... | collective-permute-start | bytes 589832 | tf_op jit(solution)/shard_map/ppermute | solution.py:454
  195.4 17.1 %collective-permute-start.22 = (bf16[1,32,1152]{2,1,0:T(8,128)(2,1)S(1)}, bf16[1,32,1152]{2,1,0:T(8,128)(2,1)S(1)}, u32[]{:S(2)}, u32[]{:S(2)}) collective-permute-start(bf16[1,32,1152]{2,1,0:T(8,128)(2,1)S(1)} %get-tuple-element.144), channel_id=1, source_target_pairs={{0,8},{2,10},{4,12},{6,14},{8,0},{10,2},{12,4},{14,6},{16,24},{18,... | collective-permute-start | bytes 221192 | tf_op jit(solution)/shard_map/ppermute | solution.py:454
  200.9 14.9 %collective-permute-start.23 = (bf16[1,32,1152]{2,1,0:T(8,128)(2,1)S(1)}, bf16[1,32,1152]{2,1,0:T(8,128)(2,1)S(1)}, u32[]{:S(2)}, u32[]{:S(2)}) collective-permute-start(bf16[1,32,1152]{2,1,0:T(8,128)(2,1)S(1)} %get-tuple-element.146), channel_id=1, source_target_pairs={{0,16},{2,18},{4,20},{6,22},{8,24},{10,26},{12,28},{14,30},{16,0},... | collective-permute-start | bytes 221192 | tf_op jit(solution)/shard_map/ppermute | solution.py:454
  208.4 7.4 %collective-permute-start.24 = (bf16[1,32,1152]{2,1,0:T(8,128)(2,1)S(1)}, bf16[1,32,1152]{2,1,0:T(8,128)(2,1)S(1)}, u32[]{:S(2)}, u32[]{:S(2)}) collective-permute-start(bf16[1,32,1152]{2,1,0:T(8,128)(2,1)S(1)} %get-tuple-element.145), channel_id=1, source_target_pairs={{0,24},{2,26},{4,28},{6,30},{8,16},{10,18},{12,20},{14,22},{16,8},... | collective-permute-start | bytes 221192 | tf_op jit(solution)/shard_map/ppermute | solution.py:454
  218.5 3.6 %collective-permute-start.45 = (f32[8,128]{1,0:T(8,128)S(1)}, f32[8,128]{1,0:T(8,128)S(1)}, u32[]{:S(2)}, u32[]{:S(2)}) collective-permute-start(f32[8,128]{1,0:T(8,128)S(1)} %add.28), channel_id=1, source_target_pairs={{0,2},{2,0},{4,6},{6,4},{8,10},{10,8},{12,14},{14,12},{16,18},{18,... | collective-permute-start | bytes 12296 | tf_op jit(solution)/shard_map/ppermute | solution.py:454
  222.2 3.6 %collective-permute-start.46 = (f32[8,128]{1,0:T(8,128)S(1)}, f32[8,128]{1,0:T(8,128)S(1)}, u32[]{:S(2)}, u32[]{:S(2)}) collective-permute-start(f32[8,128]{1,0:T(8,128)S(1)} %add.29), channel_id=1, source_target_pairs={{0,4},{2,6},{4,0},{6,2},{8,12},{10,14},{12,8},{14,10},{16,20},{18,... | collective-permute-start | bytes 12296 | tf_op jit(solution)/shard_map/ppermute | solution.py:454
  225.8 3.6 %collective-permute-start.47 = (f32[8,128]{1,0:T(8,128)S(1)}, f32[8,128]{1,0:T(8,128)S(1)}, u32[]{:S(2)}, u32[]{:S(2)}) collective-permute-start(f32[8,128]{1,0:T(8,128)S(1)} %add.30), channel_id=1, source_target_pairs={{0,8},{2,10},{4,12},{6,14},{8,0},{10,2},{12,4},{14,6},{16,24},{18,... | collective-permute-start | bytes 12296 | tf_op jit(solution)/shard_map/ppermute | solution.py:454
  229.4 4.5 %collective-permute-start.48 = (f32[8,128]{1,0:T(8,128)S(1)}, f32[8,128]{1,0:T(8,128)S(1)}, u32[]{:S(2)}, u32[]{:S(2)}) collective-permute-start(f32[8,128]{1,0:T(8,128)S(1)} %add.31), channel_id=1, source_target_pairs={{0,16},{2,18},{4,20},{6,22},{8,24},{10,26},{12,28},{14,30},{16,0},... | collective-permute-start | bytes 12296 | tf_op jit(solution)/shard_map/ppermute | solution.py:454
  (66 other events, 499.6 us)
